TPU v7x, 256 devices: a whole 4x4x8 slice. The times are simulated.
256 devices in a mesh: comp: 8 (over y, core), lat: 32 (over x, z).
Axes of the slice: x: 4, y: 4, z: 8, core: 2. Of those that a mesh axis runs over, the one named last changes fastest.
Arguments:
- spectra_in: float32 [8, 36, 196608], P(None, None, ('comp', 'lat')), may hold values from 0 to 2
- group_speed: float32 [8, 256, 1024], P('comp', 'lat'), may hold values from 0.3 to 0.9
- turn_rate: float32 [8, 256, 1024], P('comp', 'lat'), may hold values from -0.9 to 0.9
- sea_mask: int32 [256, 1024], P('lat'), may hold values from 0 to 1, as said below
- sea_cell: int32 [196608], P('lat'), may hold values from 0 to 8191, as said below
- slab_counts: int32 [32], replicated, may hold values from 3072 to 6144, as said below
Outputs:
- spectra_out: float32 [8, 36, 196608], P(None, None, ('comp', 'lat'))
Inputs may be any that keep to these rules, and one draw needn't show every extreme that they name: `sea_mask`: 1 at sea cells, 0 at land cells; slab l has slab_counts[l] sea cells. `sea_cell`: entries l * 6144 + p for p below slab_counts[l] are the indices (row in slab * 1024 + column) of slab l's sea cells in increasing order; the other entries of the slab name land cells. `slab_counts`: one slab holds exactly 6144 sea points and another exactly 3072.
All inputs are finite; a program needn't handle non-finite values.
Results may differ from a plain program's by a relative error of at most 0.0003.
Values sent between devices are 32-bit elements; how exact they have to be, the bound alone decides.
A program may use at most 128 MiB of HBM per device.

v0:
```python
import math

import jax
import jax.numpy as jnp
from jax import lax
from jax.sharding import PartitionSpec as P

SUBSTEPS = 2


def extended(cells, sides, width):
    for axis, dim in sides:
        count = lax.axis_size(axis)
        ends = count - 1
        head = lax.slice_in_dim(cells, 0, width, axis=dim)
        tail = lax.slice_in_dim(cells, cells.shape[dim] - width, cells.shape[dim], axis=dim)
        cells = jnp.concatenate(
            [
                lax.ppermute(tail, axis, [(i, (i + 1) % count) for i in range(ends)]),
                cells,
                lax.ppermute(head, axis, [((i + 1) % count, i) for i in range(ends)]),
            ],
            axis=dim,
        )
    return cells


def quickest(padded, courant, axis_dim):
    extent = padded.shape[axis_dim] - 4

    def segment(start_at, count):
        return lax.slice_in_dim(padded, start_at, start_at + count, axis=axis_dim)

    west_far = segment(0, extent + 1)
    west_near = segment(1, extent + 1)
    east_near = segment(2, extent + 1)
    east_far = segment(3, extent + 1)
    curvature = jnp.where(
        courant >= 0.0,
        east_near - 2.0 * west_near + west_far,
        east_far - 2.0 * east_near + west_near,
    )
    face_value = (
        0.5 * (west_near + east_near)
        - 0.5 * courant * (east_near - west_near)
        - (1.0 - courant * courant) / 6.0 * curvature
    )
    fluxes = courant * face_value
    return segment(2, extent) - (
        lax.slice_in_dim(fluxes, 1, extent + 1, axis=axis_dim)
        - lax.slice_in_dim(fluxes, 0, extent, axis=axis_dim)
    )


def sweep_x(energy, speed, sea_weight, cosines):
    courant = speed[:, None] * cosines[None, :, None, None]
    c_padded = jnp.pad(courant, ((0, 0), (0, 0), (0, 0), (1, 1)))
    w_padded = jnp.pad(sea_weight, ((0, 0), (0, 0), (1, 1)))[:, None]
    face_c = 0.5 * (c_padded[..., :-1] + c_padded[..., 1:]) * w_padded[..., :-1] * w_padded[..., 1:]
    padded = jnp.pad(energy, ((0, 0), (0, 0), (0, 0), (2, 2)))
    return quickest(padded, face_c, 3)


def sweep_y(energy_ext, speed, sea_weight, sines):
    row_total = energy_ext.shape[2]
    courant = speed[:, None] * sines[None, :, None, None]
    weight = sea_weight[:, None]
    face_c = (
        0.5
        * (courant[:, :, 1 : row_total - 2] + courant[:, :, 2 : row_total - 1])
        * weight[:, :, 1 : row_total - 2]
        * weight[:, :, 2 : row_total - 1]
    )
    return quickest(energy_ext, face_c, 2)


def sweep_theta(energy, turn, sea_weight, cosines):
    courant = (turn * sea_weight)[:, None] * cosines[None, :, None, None]
    c_padded = jnp.concatenate([courant[:, -1:], courant, courant[:, :1]], axis=1)
    face_c = 0.5 * (c_padded[:, :-1] + c_padded[:, 1:])
    padded = jnp.concatenate([energy[:, -2:], energy, energy[:, :2]], axis=1)
    return quickest(padded, face_c, 1)


def per_device(spectra_in, group_speed, turn_rate, sea_mask, sea_cell, slab_counts):
    comp_count = lax.axis_size("comp")
    lat_count = lax.axis_size("lat")
    devices = comp_count * lat_count
    device_id = lax.axis_index("comp") * lat_count + lax.axis_index("lat")
    lat_id = lax.axis_index("lat")
    freq_all, dir_count, slot_count = spectra_in.shape
    freq_own, row_count, columns = group_speed.shape
    sea_most = sea_cell.shape[0]
    bucket = sea_most // devices
    cell_count = row_count * columns
    slab_ends = jnp.cumsum(slab_counts)
    slab_starts = slab_ends - slab_counts
    highest = lax.Precision.HIGHEST
    first_pos = (slab_starts - device_id + devices - 1) // devices
    first_wide = jnp.broadcast_to(first_pos[:, None], (lat_count, bucket)).reshape(-1)
    ends_wide = jnp.broadcast_to(slab_ends[:, None], (lat_count, bucket)).reshape(-1)
    lane_wide = jnp.broadcast_to(
        jnp.arange(bucket, dtype=jnp.int32)[None, :], (lat_count, bucket)
    ).reshape(-1)
    wanted = first_wide + lane_wide
    column_ok = device_id + devices * wanted < ends_wide
    slot_ids = jnp.arange(slot_count, dtype=jnp.int32)
    selector = ((slot_ids[:, None] == wanted[None, :]) & column_ok[None, :]).astype(jnp.float32)
    packed = jnp.einsum(
        "fdk,kq->fdq", spectra_in, selector, precision=highest, preferred_element_type=jnp.float32
    )
    packed = packed.reshape(freq_all, dir_count, 1, lat_count, bucket)
    received = lax.all_to_all(
        lax.all_to_all(packed, "comp", split_axis=0, concat_axis=2, tiled=True),
        "lat",
        split_axis=3,
        concat_axis=3,
        tiled=True,
    )
    own_start = slab_starts[lat_id]
    own_count = slab_counts[lat_id]
    rotate = own_start % devices
    source_ids = jnp.arange(devices, dtype=jnp.int32)
    leading = (source_ids < rotate)[None, None, None, :]
    zero_lane = jnp.zeros((freq_own, dir_count, 1, devices), jnp.float32)
    spread = received.reshape(freq_own, dir_count, devices, bucket).transpose(0, 1, 3, 2)
    lifted = jnp.where(
        leading,
        jnp.concatenate([zero_lane, spread], axis=2),
        jnp.concatenate([spread, zero_lane], axis=2),
    )
    ordered = lax.dynamic_slice_in_dim(
        lifted.reshape(freq_own, dir_count, (bucket + 1) * devices), rotate, sea_most, axis=2
    )
    padded_points = jnp.concatenate(
        [ordered, jnp.zeros((freq_own, dir_count, columns), jnp.float32)], axis=2
    )
    cell_padded = jnp.concatenate([sea_cell, jnp.full((columns,), -1, jnp.int32)])
    row_sums = jnp.sum(sea_mask, axis=1)
    row_offsets = jnp.cumsum(row_sums) - row_sums
    column_ids = jnp.arange(columns, dtype=jnp.int32)

    def row_matrix(row_index):
        offset = row_offsets[row_index]
        window_cells = lax.dynamic_slice_in_dim(cell_padded, offset, columns)
        live_slot = offset + column_ids < own_count
        matrix = (
            (window_cells[:, None] == row_index * columns + column_ids[None, :])
            & live_slot[:, None]
        ).astype(jnp.float32)
        return (matrix, offset)

    def place_row(row_index, grid_now):
        matrix, offset = row_matrix(row_index)
        window = lax.dynamic_slice_in_dim(padded_points, offset, columns, axis=2)
        row_values = jnp.einsum(
            "fdp,pc->fdc", window, matrix, precision=highest, preferred_element_type=jnp.float32
        )
        return lax.dynamic_update_slice_in_dim(grid_now, row_values, row_index * columns, axis=2)

    field_grid = lax.fori_loop(
        0, row_count, place_row, jnp.zeros((freq_own, dir_count, cell_count), jnp.float32)
    )
    energy = field_grid.reshape(freq_own, dir_count, row_count, columns)
    angles = jnp.arange(dir_count, dtype=jnp.float32) * (2.0 * math.pi / dir_count)
    cosines = jnp.cos(angles)
    sines = jnp.sin(angles)
    sea_weight = sea_mask.astype(jnp.float32)[None]
    fields = jnp.stack([group_speed, turn_rate, sea_weight])
    rim_depth = 2 * SUBSTEPS
    statics = extended(fields, (("lat", 2),), rim_depth)

    def rows_now(extra):
        window = lax.slice_in_dim(statics, rim_depth - extra, rim_depth + row_count + extra, axis=2)
        return (window[0], window[1], window[2])

    own_speed, own_turn, own_weight = rows_now(0)
    wide_speed, wide_turn, wide_weight = rows_now(2)
    for substep in range(SUBSTEPS):
        energy = sweep_x(energy, own_speed, own_weight, cosines)
        energy_ext = extended(energy, (("lat", 2),), 2)
        energy = sweep_y(energy_ext, wide_speed, wide_weight, sines)
        energy = sweep_theta(energy, own_turn, own_weight, cosines)
    flat_grid = energy.reshape(freq_own, dir_count, cell_count)

    def take_row(row_index, collected):
        matrix, offset = row_matrix(row_index)
        grid_row = lax.dynamic_slice_in_dim(flat_grid, row_index * columns, columns, axis=2)
        portion = jnp.einsum(
            "fdc,pc->fdp", grid_row, matrix, precision=highest, preferred_element_type=jnp.float32
        )
        current = lax.dynamic_slice_in_dim(collected, offset, columns, axis=2)
        return lax.dynamic_update_slice_in_dim(collected, current + portion, offset, axis=2)

    collected = lax.fori_loop(
        0, row_count, take_row, jnp.zeros((freq_own, dir_count, sea_most + columns), jnp.float32)
    )
    points_out = collected[:, :, :sea_most]
    holder = jnp.zeros((freq_own, dir_count, (bucket + 1) * devices), jnp.float32)
    holder = lax.dynamic_update_slice_in_dim(holder, points_out, rotate, axis=2).reshape(
        freq_own, dir_count, bucket + 1, devices
    )
    unrolled = jnp.where(leading, holder[:, :, 1:], holder[:, :, :-1])
    values = unrolled.transpose(0, 1, 3, 2).reshape(
        freq_own, dir_count, comp_count, lat_count, bucket
    )
    returned = lax.all_to_all(
        lax.all_to_all(values, "lat", split_axis=3, concat_axis=3, tiled=True),
        "comp",
        split_axis=2,
        concat_axis=0,
        tiled=True,
    )
    spectra_out = jnp.einsum(
        "fdq,kq->fdk",
        returned.reshape(freq_all, dir_count, lat_count * bucket),
        selector,
        precision=highest,
        preferred_element_type=jnp.float32,
    )
    return spectra_out


def solution(mesh):
    in_specs = (
        P(None, None, ("comp", "lat")),
        P("comp", "lat", None),
        P("comp", "lat", None),
        P("lat", None),
        P("lat"),
        P(),
    )
    out_specs = P(None, None, ("comp", "lat"))
    return jax.shard_map(
        per_device, mesh=mesh, in_specs=in_specs, out_specs=out_specs, check_vma=False
    )
```

profile of v0, /device:TPU:1, one launch (start us, length us, event | category | flops | bytes accessed | tf_op | source)
XLA Modules:
  0.0 391.2 jit_solution(10995612735044304133)
XLA Ops:
  2.0 2.6 fusion.43
  4.6 2.0 copy.38
  6.7 4.7 %reshape.323 = f32[8,1,27648]{2,1,0:T(1,128)} reshape(f32[8,1,32,24,36]{4,3,2,1,0:T(8,128)S(1)} %bitcast.122) | data formatting | bytes 1769472
  11.4 6.8 %all-to-all-start = ((f32[8,1,27648]{2,1,0:T(1,128)}), f32[8,1,27648]{2,1,0:T(1,128)S(1)}, u32[]{:S(2)}, u32[]{:S(2)}) async-start(f32[8,1,27648]{2,1,0:T(1,128)} %reshape.323), calls=%async_computation | async-start | bytes 1769472 | tf_op jit(solution)/shard_map/all_to_all | solution.py:114
  18.4 2.8 collective-permute-start
  23.6 8.0 %all-to-all-done = f32[8,1,27648]{2,1,0:T(1,128)S(1)} async-done(((f32[8,1,27648]{2,1,0:T(1,128)}), f32[8,1,27648]{2,1,0:T(1,128)S(1)}, u32[]{:S(2)}, u32[]{:S(2)}) %all-to-all-start) | async-done | bytes 884768 | tf_op jit(solution)/shard_map/all_to_all | solution.py:114
  32.2 3.9 %reduce.2 = f32[8,27648]{1,0:T(8,128)} reduce(f32[8,1,27648]{2,1,0:T(1,128)S(1)} %all-to-all-done, f32[]{:T(128)} %broadcast.313), dimensions={1}, to_apply=%all_to_all.30.reduce_sub_computation | reduce | bytes 1769476 | tf_op jit(solution)/shard_map/all_to_all | solution.py:114
  36.1 5.2 %reshape.324 = f32[8,1,32,24,36]{4,3,2,1,0:T(8,128)S(1)} reshape(f32[8,27648]{1,0:T(8,128)} %reduce.2) | data formatting | bytes 1769472
  41.4 2.0 copy_bitcast_fusion.3
  43.4 6.1 %reshape.325 = f32[32,1,6912]{2,1,0:T(1,128)} reshape(f32[32,1,8,24,36]{4,3,2,1,0:T(8,128)} %copy_bitcast_fusion.3) | data formatting | bytes 1769472
  49.5 10.5 %all-to-all-start.1 = ((f32[32,1,6912]{2,1,0:T(1,128)}), f32[32,1,6912]{2,1,0:T(1,128)S(1)}, u32[]{:S(2)}, u32[]{:S(2)}) async-start(f32[32,1,6912]{2,1,0:T(1,128)} %reshape.325), calls=%async_computation.1 | async-start | bytes 1769472 | tf_op jit(solution)/shard_map/all_to_all | solution.py:113
  68.3 12.9 %all-to-all-done.1 = f32[32,1,6912]{2,1,0:T(1,128)S(1)} async-done(((f32[32,1,6912]{2,1,0:T(1,128)}), f32[32,1,6912]{2,1,0:T(1,128)S(1)}, u32[]{:S(2)}, u32[]{:S(2)}) %all-to-all-start.1) | async-done | bytes 884768 | tf_op jit(solution)/shard_map/all_to_all | solution.py:113
  81.3 2.8 reduce.3
  84.0 5.7 %reshape.326 = f32[32,1,8,24,36]{4,3,2,1,0:T(8,128)} reshape(f32[32,6912]{1,0:T(8,128)S(1)} %reduce.3) | data formatting | bytes 1769472
  89.8 4.8 %copy.25 = f32[1,36,8,32,24]{3,2,4,1,0:T(8,128)S(1)} copy(f32[1,36,8,32,24]{1,4,2,0,3:T(8,128)} %bitcast.119) | data formatting | bytes 1769472 | tf_op jit(solution)/shard_map/all_to_all | solution.py:113
  99.0 1.9 constant_dynamic-slice_fusion.1
  101.6 54.2 %while.30 = (s32[]{:T(128)}, f32[1,36,8192]{2,1,0:T(8,128)S(1)}, s32[8]{0:T(128)S(1)}, f32[1,36,7168]{2,0,1:T(1,128)S(1)}, s32[7168]{0:T(1024)}, /*index=5*/s32[...) while((s32[]{:T(128)}, f32[1,36,8192]{2,1,0:T(8,128)S(1)}, ...), condition=%wide.region_4.5_spmd.clone.clone, body=%wide.region_3.4_spmd.clone.clone.sunk | while | flops 455085056 | bytes 628961 | solution.py:161
  160.0 5.2 %collective-permute-start.2 = (f32[1,36,2,1024]{3,2,0,1:T(2,128)S(1)}, f32[1,36,2,1024]{3,2,0,1:T(2,128)S(1)}, u32[]{:S(2)}, u32[]{:S(2)}) collective-permute-start(f32[1,36,2,1024]{3,2,0,1:T(2,128)S(1)} %get-tuple-element.383), channel_id=1, source_target_pairs={{0,1},{1,2},{2,3},{3,4},{4,5},{5,6},{6,7},{7,8},{8,9},{9,10},{10,1... | collective-permute-start | bytes 884744 | tf_op jit(solution)/shard_map/ppermute | solution.py:19
  167.0 1.9 collective-permute-done.2
  168.8 4.0 %collective-permute-done.3 = f32[1,36,2,1024]{3,2,0,1:T(2,128)S(1)} collective-permute-done((f32[1,36,2,1024]{3,2,0,1:T(2,128)S(1)}, f32[1,36,2,1024]{3,2,0,1:T(2,128)S(1)}, u32[]{:S(2)}, u32[]{:S(2)}) %collective-permute-start.3) | collective-permute-done | bytes 294944 | tf_op jit(solution)/shard_map/ppermute | solution.py:21
  172.8 2.9 fusion.33
  181.0 3.3 collective-permute-start.4
  185.5 2.0 collective-permute-done.4
  187.5 4.5 %collective-permute-done.5 = f32[1,36,2,1024]{3,2,0,1:T(2,128)} collective-permute-done((f32[1,36,2,1024]{3,2,0,1:T(2,128)}, f32[1,36,2,1024]{3,2,0,1:T(2,128)}, u32[]{:S(2)}, u32[]{:S(2)}) %collective-permute-start.5) | collective-permute-done | bytes 294944 | tf_op jit(solution)/shard_map/ppermute | solution.py:21
  192.0 4.3 %fusion.26 = f32[1,36,9,1024]{3,2,0,1:T(8,128)S(1)} fusion(f32[1,36,2,1024]{3,2,0,1:T(2,128)} %collective-permute-done.5, f32[1,36,8,1024]{3,2,0,1:T(8,128)S(1)} %fusion.66, f32[1,36,2,1024]{3,2,0,1:T(2,128)} %collective-permute-done.4, f32[9,1024]{1,0:T(8,128)} %get-tuple-element.386, f32[9,1024]{1,0:T(8,128)} %get-tuple-element.385, ...), kind=kLoop, calls=%fused_computation.33 | loop fusion | flops 8957952 | bytes 5824512 | tf_op jit(solution)/shard_map/mul | solution.py:48
  199.4 67.1 %while.31 = (s32[]{:T(128)}, f32[1,36,7168]{2,1,0:T(8,128)S(1)}, s32[8]{0:T(128)S(1)}, f32[1,36,8192]{2,1,0:T(8,128)S(1)}, s32[7168]{0:T(1024)}, /*index=5*/s32[...) while((s32[]{:T(128)}, f32[1,36,7168]{2,1,0:T(8,128)S(1)}, ...), condition=%wide.region_6.7_spmd.clone.clone, body=%wide.region_5.6_spmd.clone.clone.sunk | while | flops 455121920 | bytes 792805 | solution.py:195
  204.0 2.2 fusion.100
  212.2 2.2 fusion.100
  220.6 2.2 fusion.100
  229.0 2.2 fusion.100
  237.4 2.2 fusion.100
  245.8 2.2 fusion.100
  254.3 2.2 fusion.100
  262.7 2.2 fusion.100
  267.9 11.9 %dynamic_update_slice.17 = f32[1,36,6400]{2,0,1:T(1,128)S(1)} dynamic-update-slice(f32[1,36,6400]{2,0,1:T(1,128)S(1)} %broadcast_in_dim.45, f32[1,36,6144]{2,0,1:T(1,128)S(1)} %copy.28, s32[]{:T(128)} %constant.147.clone.1, s32[]{:T(128)} %constant.147.clone.1, s32[]{:T(128)S(6)} %select_n.94) | dynamic-update-slice | bytes 1769476 | tf_op jit(solution)/shard_map/dynamic_update_slice | solution.py:200
  279.9 2.2 reduce.1
  283.3 2.3 reshape.312
  285.6 4.5 %copy.29 = f32[1,36,8,32,24]{1,4,2,0,3:T(8,128)} copy(f32[1,36,8,32,24]{3,2,4,1,0:T(8,128)S(1)} %reshape.312) | data formatting | bytes 1769472 | tf_op jit(solution)/shard_map/reshape | solution.py:204
  290.1 5.5 %reshape.327 = f32[32,1,6912]{2,1,0:T(1,128)S(1)} reshape(f32[32,1,8,24,36]{4,3,2,1,0:T(8,128)} %bitcast.120) | data formatting | bytes 1769472
  295.6 36.1 %all_to_all.43 = f32[32,1,6912]{2,1,0:T(1,128)S(1)} all-to-all(f32[32,1,6912]{2,1,0:T(1,128)S(1)} %reshape.327), channel_id=1, replica_groups=mesh['comp'=8,'lat'=32] {'lat'}, dimensions={0} | all-to-all | bytes 1769472 | tf_op jit(solution)/shard_map/all_to_all | solution.py:208
  331.7 3.9 reduce.4
  335.5 5.2 %reshape.328 = f32[32,1,8,24,36]{4,3,2,1,0:T(8,128)S(1)} reshape(f32[32,6912]{1,0:T(8,128)} %reduce.4) | data formatting | bytes 1769472
  340.7 1.8 copy_bitcast_fusion.2
  342.6 5.2 %reshape.329 = f32[8,1,27648]{2,1,0:T(1,128)S(1)} reshape(f32[8,1,32,24,36]{4,3,2,1,0:T(8,128)} %copy_bitcast_fusion.2) | data formatting | bytes 1769472
  347.7 23.8 %all_to_all.44 = f32[8,1,27648]{2,1,0:T(1,128)S(1)} all-to-all(f32[8,1,27648]{2,1,0:T(1,128)S(1)} %reshape.329), channel_id=1, replica_groups=mesh['comp'=8,'lat'=32] {'comp'}, dimensions={0} | all-to-all | bytes 1769472 | tf_op jit(solution)/shard_map/all_to_all | solution.py:207
  371.6 2.8 reduce.5
  374.4 5.7 %reshape.330 = f32[8,1,32,24,36]{4,3,2,1,0:T(8,128)} reshape(f32[8,27648]{1,0:T(8,128)S(1)} %reduce.5) | data formatting | bytes 1769472
  380.1 9.5 %fusion.39 = f32[8,36,768]{2,1,0:T(8,128)S(1)} fusion(f32[8,36,768]{1,2,0:T(8,128)} %bitcast.121, s32[768]{0:T(1024)S(1)} %add.291, pred[768]{0:T(1024)(128)(4,1)S(1)} %add_compare_fusion), kind=kOutput, calls=%fused_computation.56 | convolution fusion | flops 2039611392 | bytes 1773312 | tf_op jit(solution)/shard_map/fdq,kq->fdk/dot_general | solution.py:214
  (208 shorter events, 106.9 us)
Async XLA Ops:
  0.0 2.0 copy-start
  11.4 6.8 %copy-start.23 = (s32[8,1024]{1,0:T(8,128)S(1)}, s32[8,1024]{1,0:T(8,128)}, u32[]{:S(2)}) copy-start(s32[8,1024]{1,0:T(8,128)} %param.13) | copy-start | bytes 98308
  11.4 7.0 %copy-start.7 = (f32[1,8,1024]{2,1,0:T(8,128)S(1)}, f32[1,8,1024]{2,1,0:T(8,128)}, u32[]{:S(2)}) copy-start(f32[1,8,1024]{2,1,0:T(8,128)} %param.11) | copy-start | bytes 98308
  11.4 7.0 %copy-start.9 = (f32[1,8,1024]{2,1,0:T(8,128)S(1)}, f32[1,8,1024]{2,1,0:T(8,128)}, u32[]{:S(2)}) copy-start(f32[1,8,1024]{2,1,0:T(8,128)} %param.12) | copy-start | bytes 98308
  11.4 20.2 %all-to-all-start = ((f32[8,1,27648]{2,1,0:T(1,128)}), f32[8,1,27648]{2,1,0:T(1,128)S(1)}, u32[]{:S(2)}, u32[]{:S(2)}) async-start(f32[8,1,27648]{2,1,0:T(1,128)} %reshape.323), calls=%async_computation | async-start | bytes 1769472 | tf_op jit(solution)/shard_map/all_to_all | solution.py:114
  18.3 49.3 %copy-start.11 = (f32[1,1,8,1024]{3,2,1,0:T(8,128)}, f32[1,1,8,1024]{3,2,1,0:T(8,128)S(1)}, u32[]{:S(2)}) copy-start(f32[1,1,8,1024]{3,2,1,0:T(8,128)S(1)} %get-tuple-element.391) | copy-start | bytes 98308
  18.4 49.2 %collective-permute-start = (f32[3,1,4,1024]{3,2,1,0:T(4,128)S(1)}, f32[3,1,4,1024]{3,2,1,0:T(4,128)S(1)}, u32[]{:S(2)}, u32[]{:S(2)}) collective-permute-start(f32[3,1,4,1024]{3,2,1,0:T(4,128)S(1)} %get-tuple-element.387), channel_id=1, source_target_pairs={{0,1},{1,2},{2,3},{3,4},{4,5},{5,6},{6,7},{7,8},{8,9},{9,10},{10,1... | collective-permute-start | bytes 147464 | tf_op jit(solution)/shard_map/ppermute | solution.py:19
  21.2 46.4 %collective-permute-start.1 = (f32[3,1,4,1024]{3,2,1,0:T(4,128)S(1)}, f32[3,1,4,1024]{3,2,1,0:T(4,128)S(1)}, u32[]{:S(2)}, u32[]{:S(2)}) collective-permute-start(f32[3,1,4,1024]{3,2,1,0:T(4,128)S(1)} %get-tuple-element.388), channel_id=1, source_target_pairs={{1,0},{2,1},{3,2},{4,3},{5,4},{6,5},{7,6},{8,7},{9,8},{10,9},{11,1... | collective-permute-start | bytes 147464 | tf_op jit(solution)/shard_map/ppermute | solution.py:21
  49.5 31.8 %all-to-all-start.1 = ((f32[32,1,6912]{2,1,0:T(1,128)}), f32[32,1,6912]{2,1,0:T(1,128)S(1)}, u32[]{:S(2)}, u32[]{:S(2)}) async-start(f32[32,1,6912]{2,1,0:T(1,128)} %reshape.325), calls=%async_computation.1 | async-start | bytes 1769472 | tf_op jit(solution)/shard_map/all_to_all | solution.py:113
  63.9 2.5 copy-start.25
  63.9 3.1 copy-start.24
  67.6 22.1 %copy-start.19 = (f32[3,1,4,1024]{3,2,1,0:T(4,128)}, f32[3,1,4,1024]{3,2,1,0:T(4,128)S(1)}, u32[]{:S(2)}) copy-start(f32[3,1,4,1024]{3,2,1,0:T(4,128)S(1)} %collective-permute-done) | copy-start | bytes 147460
  67.6 22.1 %copy-start.21 = (f32[3,1,4,1024]{3,2,1,0:T(4,128)}, f32[3,1,4,1024]{3,2,1,0:T(4,128)S(1)}, u32[]{:S(2)}) copy-start(f32[3,1,4,1024]{3,2,1,0:T(4,128)S(1)} %collective-permute-done.1) | copy-start | bytes 147460
  100.8 0.8 copy-start.26
  156.7 1.3 copy-start.4
  156.7 1.3 copy-start.13
  156.7 1.3 copy-start.14
  159.3 7.3 %copy-start.8 = (f32[1,8,1024]{2,1,0:T(8,128)S(1)}, f32[1,8,1024]{2,1,0:T(8,128)}, u32[]{:S(2)}) copy-start(f32[1,8,1024]{2,1,0:T(8,128)} %param.11) | copy-start | bytes 98308
  159.4 7.3 %copy-start.10 = (f32[1,8,1024]{2,1,0:T(8,128)S(1)}, f32[1,8,1024]{2,1,0:T(8,128)}, u32[]{:S(2)}) copy-start(f32[1,8,1024]{2,1,0:T(8,128)} %param.12) | copy-start | bytes 98308
  159.4 7.3 %copy-start.12 = (f32[1,1,8,1024]{3,2,1,0:T(8,128)S(1)}, f32[1,1,8,1024]{3,2,1,0:T(8,128)}, u32[]{:S(2)}) copy-start(f32[1,1,8,1024]{3,2,1,0:T(8,128)} %copy-done.11) | copy-start | bytes 98308
  159.4 7.3 %copy-start.20 = (f32[3,1,4,1024]{3,2,1,0:T(4,128)S(1)}, f32[3,1,4,1024]{3,2,1,0:T(4,128)}, u32[]{:S(2)}) copy-start(f32[3,1,4,1024]{3,2,1,0:T(4,128)} %copy-done.19) | copy-start | bytes 147460
  159.4 7.3 %copy-start.22 = (f32[3,1,4,1024]{3,2,1,0:T(4,128)S(1)}, f32[3,1,4,1024]{3,2,1,0:T(4,128)}, u32[]{:S(2)}) copy-start(f32[3,1,4,1024]{3,2,1,0:T(4,128)} %copy-done.21) | copy-start | bytes 147460
  160.0 8.9 %collective-permute-start.2 = (f32[1,36,2,1024]{3,2,0,1:T(2,128)S(1)}, f32[1,36,2,1024]{3,2,0,1:T(2,128)S(1)}, u32[]{:S(2)}, u32[]{:S(2)}) collective-permute-start(f32[1,36,2,1024]{3,2,0,1:T(2,128)S(1)} %get-tuple-element.383), channel_id=1, source_target_pairs={{0,1},{1,2},{2,3},{3,4},{4,5},{5,6},{6,7},{7,8},{8,9},{9,10},{10,1... | collective-permute-start | bytes 884744 | tf_op jit(solution)/shard_map/ppermute | solution.py:19
  165.2 7.6 %copy-start.5 = (f32[9,1024]{1,0:T(8,128)S(1)}, f32[9,1024]{1,0:T(8,128)}, u32[]{:S(2)}) copy-start(f32[9,1024]{1,0:T(8,128)} %get-tuple-element.385) | copy-start | bytes 110596
  165.2 7.6 %copy-start.6 = (f32[9,1024]{1,0:T(8,128)S(1)}, f32[9,1024]{1,0:T(8,128)}, u32[]{:S(2)}) copy-start(f32[9,1024]{1,0:T(8,128)} %get-tuple-element.386) | copy-start | bytes 110596
  165.2 7.6 %collective-permute-start.3 = (f32[1,36,2,1024]{3,2,0,1:T(2,128)S(1)}, f32[1,36,2,1024]{3,2,0,1:T(2,128)S(1)}, u32[]{:S(2)}, u32[]{:S(2)}) collective-permute-start(f32[1,36,2,1024]{3,2,0,1:T(2,128)S(1)} %get-tuple-element.384), channel_id=1, source_target_pairs={{1,0},{2,1},{3,2},{4,3},{5,4},{6,5},{7,6},{8,7},{9,8},{10,9},{11,1... | collective-permute-start | bytes 884744 | tf_op jit(solution)/shard_map/ppermute | solution.py:21
  175.8 1.3 copy-start.2
  175.8 1.3 copy-start.15
  175.8 1.3 copy-start.17
  181.0 6.5 %collective-permute-start.4 = (f32[1,36,2,1024]{3,2,0,1:T(2,128)}, f32[1,36,2,1024]{3,2,0,1:T(2,128)}, u32[]{:S(2)}, u32[]{:S(2)}) collective-permute-start(f32[1,36,2,1024]{3,2,0,1:T(2,128)} %get-tuple-element.377), channel_id=1, source_target_pairs={{0,1},{1,2},{2,3},{3,4},{4,5},{5,6},{6,7},{7,8},{8,9},{9,10},{10,1... | collective-permute-start | bytes 884744 | tf_op jit(solution)/shard_map/ppermute | solution.py:19
  184.2 7.8 %collective-permute-start.5 = (f32[1,36,2,1024]{3,2,0,1:T(2,128)}, f32[1,36,2,1024]{3,2,0,1:T(2,128)}, u32[]{:S(2)}, u32[]{:S(2)}) collective-permute-start(f32[1,36,2,1024]{3,2,0,1:T(2,128)} %get-tuple-element.378), channel_id=1, source_target_pairs={{1,0},{2,1},{3,2},{4,3},{5,4},{6,5},{7,6},{8,7},{9,8},{10,9},{11,1... | collective-permute-start | bytes 884744 | tf_op jit(solution)/shard_map/ppermute | solution.py:21
  196.3 1.3 copy-start.3
  196.3 1.3 copy-start.16
  196.3 1.3 copy-start.18
  198.7 0.7 copy-start.27
  380.1 10.7 %copy-start.1 = (f32[8,36,768]{2,0,1:T(8,128)S(1)}, f32[8,36,768]{2,0,1:T(8,128)}, u32[]{:S(2)}) copy-start(f32[8,36,768]{2,0,1:T(8,128)} %param.10) | copy-start | bytes 2654212
where the time goes:
time: 398 us; the launch traced here: 391 us
  local copies, waits for them, and re-layouts  128 us (32%)
  blocking collectives  59.9 us (15%)
  other arithmetic  58.5 us (15%)
  matrix products  43.5 us (11%)
  waiting for transfers between devices  33.2 us (8%)
  starting transfers between devices  32.9 us (8%)
  loops' own time  32.2 us (8%)
    unnamed x67, local copies, waits for them, and re-layouts  51.2 us
    all_to_all x1, blocking collectives, per_device(): lax.all_to_all(values, 'lat', split_axis=3, concat_axis=3, tiled=True)  36.1 us
    all_to_all x1, blocking collectives, per_device(): lax.all_to_all(lax.all_to_all(values, 'lat', split_axis=3, concat_axis=3,...  23.8 us
    lt x16, other arithmetic, row_matrix(): live_slot = offset + column_ids < own_count  20.6 us
    dot_general x8, matrix products, take_row(): jnp.einsum('fdc,pc->fdp', grid_row, matrix, precision=highest, preferred_...  17.7 us
    another operation x1, loops' own time, per_device(): lax.fori_loop(0, row_count, place_row, jnp.zeros((freq_own, dir_count, ce...  16.3 us
    another operation x1, loops' own time, per_device(): lax.fori_loop(0, row_count, take_row, jnp.zeros((freq_own, dir_count, sea...  15.9 us
    dot_general x8, matrix products, place_row(): jnp.einsum('fdp,pc->fdc', window, matrix, precision=highest, preferred_el...  13.7 us
  transfers between devices with their start and end apart: 8, of which 6 were waited for; matrix products, arithmetic and copies ran while one was open for 7% of the time, Pallas kernels for 0%

commit v1 on v0

v1 whole, which is shorter than its diff:
```python
import math

import jax
import jax.numpy as jnp
import numpy as np
from jax import lax
from jax.experimental import pallas as pl
from jax.experimental.pallas import tpu as pltpu
from jax.sharding import PartitionSpec as P

NC = 8
NL = 32
ND = 36
SLOTS = 768
BUCKET = 24
ROWS = 8
FOLD = 5
TILES = 7
LAST = ND - 1
CHUNKS = ((32, 4), (0, 8), (8, 8), (16, 8), (24, 8))
GROUPS = ((0, 2), (2, 2), (4, 3))
PIECES = ((0, 32), (32, 4))
SIN_POS = 19

ANGLES = np.arange(ND, dtype=np.float32) * np.float32(2.0 * math.pi / ND)
COS = np.cos(ANGLES).astype(np.float32)
SIN = np.sin(ANGLES).astype(np.float32)
TURN = (0.5 * (COS + np.roll(COS, -1))).astype(np.float32)
assert (SIN[:SIN_POS] >= 0).all() and (SIN[SIN_POS:] < 0).all()

SLOT_TILES = ((0,), (0, 1), (0, 1, 2), (1, 2, 3), (1, 2, 3, 4), (2, 3, 4, 5), (2, 3, 4, 5))
POINT_TILES = tuple(
    tuple(range(max(0, 4 * v - 20) // 8, min(2, (4 * v + 3) // 8) + 1)) for v in range(ROWS)
)
ROW_TILES = tuple(tuple(range(2 * u, min(7, 2 * u + 6) + 1)) for u in range(3))


def lanes(values, index):
    return jnp.take_along_axis(values, index, axis=1)


def sublanes(values, index):
    return jnp.take_along_axis(values, index, axis=0)


def iotas():
    return (
        lax.broadcasted_iota(jnp.int32, (8, 128), 0),
        lax.broadcasted_iota(jnp.int32, (8, 128), 1),
    )


def swap_blocks(parts, block_masks, turns):
    rolled = []
    for k in range(FOLD):
        diagonal = parts[(FOLD - 1 + k) % FOLD]
        for b in range(FOLD - 1):
            diagonal = jnp.where(block_masks[b], parts[(b + k) % FOLD], diagonal)
        rolled.append(diagonal if k == 0 else lanes(diagonal, turns[k]))
    outs = []
    for a in range(FOLD):
        value = rolled[(FOLD - 1 - a) % FOLD]
        for b in range(FOLD - 1):
            value = jnp.where(block_masks[b], rolled[(b - a) % FOLD], value)
        outs.append(value)
    return outs


def flux(q, d, curvature, c):
    sixth = 1.0 / 6.0
    return c * (q + (1.0 - c) * (0.5 * d - (c * sixth + sixth) * curvature))


def sweep_x(q, c, sign, sub, lane):
    east = lanes(q, (lane + 1) & 127)
    east = jnp.where(lane == 127, sublanes(east, (sub + 1) & 7), east)
    east = jnp.where((lane == 127) & (sub == 7), 0.0, east)
    d = east - q
    side = lanes(d, (lane - sign) & 127)
    edge = lane == jnp.where(sign > 0, 0, 127)
    side = jnp.where(edge, sublanes(side, (sub - sign) & 7), side)
    side = jnp.where(edge & (sub == jnp.where(sign > 0, 0, 7)), q, side)
    curvature = (d - side) * jnp.where(sign > 0, 1.0, -1.0)
    f = flux(q, d, curvature, c)
    west = lanes(f, (lane - 1) & 127)
    west = jnp.where(lane == 0, sublanes(west, (sub - 1) & 7), west)
    return q - (f - west)


def kernel(
    spectra, speed, turn, mask, cells, counts, trig, out,
    a_buf, m_buf, r_buf, p_buf, n_buf, o_buf, x_ext, y_buf,
    spd, trn, msk, stat_halo, sx, sy,
    pack_at, put_at, put_tile, row_at, row_tile, lane_at, take_at, back_row, back_tile, w_last,
    first_send, first_recv, first_own, second_send, second_recv, second_own,
    stat_send, stat_recv, halo_send, halo_recv,
    third_send, third_recv, third_own, fourth_send, fourth_recv, fourth_own,
):
    me_c = lax.axis_index("comp")
    me_l = lax.axis_index("lat")
    sub, lane = iotas()

    def slot_of(c):
        return (c % 4) * 2 + c // 4

    def first_ends(g, peer):
        part = pl.ds(*CHUNKS[g])
        return spectra.at[part, peer, :], a_buf.at[part, slot_of(me_c), :]

    def first_local(g):
        source_ref, target_ref = first_ends(g, me_c)
        return pltpu.make_async_copy(source_ref, target_ref, first_own.at[g])

    for g in range(len(CHUNKS)):
        first_local(g).start()

    barrier = pltpu.get_barrier_semaphore()

    def greet_comp(r, carry):
        pl.semaphore_signal(
            barrier, inc=1, device_id={"comp": (me_c + r) % NC, "lat": me_l}, device_id_type=pl.DeviceIdType.MESH
        )
        return carry

    def greet_lat(r, carry):
        pl.semaphore_signal(
            barrier, inc=1, device_id={"comp": me_c, "lat": (me_l + r) % NL}, device_id_type=pl.DeviceIdType.MESH
        )
        return carry

    lax.fori_loop(1, NC, greet_comp, 0)
    lax.fori_loop(1, NL, greet_lat, 0)

    starts = [jnp.int32(0)]
    for slab in range(NL):
        starts.append(starts[-1] + counts[slab])
    own_start = jnp.int32(0)
    for slab in range(NL):
        own_start = own_start + jnp.where(slab < me_l, counts[slab], 0)

    source = ((sub & 1) * 4 + (sub >> 1)) * NL + me_l
    block = (lane * 171) >> 12
    in_block = lane - block * BUCKET
    block_masks = [block == b for b in range(FOLD)]
    turns = [None] + [
        jnp.where(lane >= BUCKET * k, lane - BUCKET * k, lane - BUCKET * k + BUCKET * FOLD) & 127
        for k in range(1, FOLD)
    ]
    for v in range(TILES):
        base = jnp.full((8, 128), starts[min(FOLD * v, NL - 1)], jnp.int32)
        for b in range(1, FOLD):
            if FOLD * v + b < NL:
                base = jnp.where(block == b, starts[FOLD * v + b], base)
        pack_at[v] = ((base - source + 255) >> 8) + in_block

    for t in range(8):
        columns = pl.ds(128 * t, 128)
        spd[pl.ds(t, 8, stride=8), :] = speed[0, :, columns]
        trn[pl.ds(t, 8, stride=8), :] = turn[0, :, columns]
        msk[pl.ds(t, 8, stride=8), :] = mask[:, columns].astype(jnp.float32)

    pl.semaphore_wait(barrier, NC - 1 + NL - 1)

    def first_copy(g, r):
        peer = (me_c + r) % NC
        source_ref, target_ref = first_ends(g, peer)
        return pltpu.make_async_remote_copy(
            src_ref=source_ref,
            dst_ref=target_ref,
            send_sem=first_send.at[g],
            recv_sem=first_recv.at[g],
            device_id={"comp": peer, "lat": me_l},
            device_id_type=pl.DeviceIdType.MESH,
        )

    for g in range(len(CHUNKS)):
        for r in range(1, NC):
            first_copy(g, r).start()

    north = {"comp": me_c, "lat": (me_l + 1) % NL}
    south = {"comp": me_c, "lat": (me_l + NL - 1) % NL}

    def stat_copy(k):
        ref = (spd, msk)[k % 2]
        row = 56 if k < 2 else 0
        return pltpu.make_async_remote_copy(
            src_ref=ref.at[pl.ds(row, 8), :],
            dst_ref=stat_halo.at[k],
            send_sem=stat_send.at[k],
            recv_sem=stat_recv.at[k],
            device_id=north if k < 2 else south,
            device_id_type=pl.DeviceIdType.MESH,
        )

    for k in range(4):
        stat_copy(k).start()

    def first_wait(g, sem):
        low, size = CHUNKS[g]
        ref = a_buf.at[pl.ds(low, size), pl.ds(0, NC - 1), :]
        return pltpu.make_async_copy(ref, ref, sem.at[g])

    for u in range(6):
        point = source + (lane + 128 * u) * 256
        slab = jnp.zeros((8, 128), jnp.int32)
        begin = jnp.zeros((8, 128), jnp.int32)
        for s in range(1, NL + 1):
            past = point >= starts[s]
            slab = jnp.where(past, s, slab)
            begin = jnp.where(past, starts[s], begin)
        nth = lane + 128 * u - ((begin - source + 255) >> 8)
        tile = (slab * 205) >> 10
        put_at[u] = ((slab - tile * FOLD) * BUCKET + nth) & 127
        put_tile[u] = jnp.where(slab < NL, tile, -1)

    ones = jnp.ones((128, 128), jnp.bfloat16)
    deep = lax.broadcasted_iota(jnp.int32, (128, 128), 0)
    wide = lax.broadcasted_iota(jnp.int32, (128, 128), 1)
    before = jnp.where(deep < wide, 1.0, 0.0).astype(jnp.bfloat16)
    above = jnp.where(wide < deep, 1.0, 0.0).astype(jnp.bfloat16)[:64, :64]
    sea = msk[...].astype(jnp.bfloat16)
    inside = jnp.dot(sea, before, preferred_element_type=jnp.float32)
    totals = jnp.dot(sea, ones, preferred_element_type=jnp.float32)
    offsets = jnp.dot(above, totals.astype(jnp.bfloat16), preferred_element_type=jnp.float32)
    inside = inside.astype(jnp.int32)
    offsets = offsets.astype(jnp.int32)
    low_source = (lane & 3) * NL + (lane >> 2)
    for v in range(ROWS):
        offset = offsets[8 * v : 8 * v + 8]
        point = offset + inside[8 * v : 8 * v + 8] + own_start
        lane_at[v] = ((point & 31) << 2) | ((point >> 5) & 3)
        point = offset + ((low_source - own_start - offset) & 127)
        row_at[v] = (point >> 8) & 7
        row_tile[v] = ((point >> 11) << 1) + (((point + own_start) >> 7) & 1)
    cell_at = []
    for u in range(3):
        even = cells[pl.ds(16 * u, 8, stride=2), :]
        odd = cells[pl.ds(16 * u + 1, 8, stride=2), :]
        for h in range(2):
            rho = (low_source + 128 * h - own_start) & 255
            cell = jnp.where(rho < 128, lanes(even, rho & 127), lanes(odd, rho & 127))
            cell_at.append(cell)
            back_row[u, h] = (cell >> 7) & 7
            back_tile[u, h] = cell >> 10
    for v in range(ROWS):
        index = row_at[v]
        which = row_tile[v]
        value = jnp.zeros((8, 128), jnp.int32)
        for u in POINT_TILES[v]:
            for h in range(2):
                value = jnp.where(which == 2 * u + h, sublanes(cell_at[2 * u + h], index), value)
        take_at[v] = value & 127

    for v in range(ROWS):
        rows = pl.ds(8 * v, 8)
        s = spd[rows, :]
        m = msk[rows, :]

        def eastward(x):
            east = lanes(x, (lane + 1) & 127)
            return jnp.where(lane == 127, sublanes(east, (sub + 1) & 7), east)

        face = 0.5 * (s + eastward(s)) * m * eastward(m)
        sx[v] = jnp.where((lane == 127) & (sub == 7), 0.0, face)
        trn[rows, :] = trn[rows, :] * m
        if v < ROWS - 1:
            after = pl.ds(8 * v + 8, 8)
            sy[v + 1] = 0.5 * (s + spd[after, :]) * m * msk[after, :]
    for k in range(4):
        stat_copy(k).wait()
    south_mask = jnp.where(me_l > 0, stat_halo[1], 0.0)
    north_mask = jnp.where(me_l < NL - 1, stat_halo[3], 0.0)
    sy[0] = 0.5 * (stat_halo[0] + spd[0:8, :]) * south_mask * msk[0:8, :]
    sy[8] = 0.5 * (stat_halo[2] + spd[56:64, :]) * north_mask * msk[56:64, :]

    def a_rows(direction):
        return [a_buf[direction, :, pl.ds(128 * u, 128)] for u in range(6)]

    def windows(direction, v, rows):
        at = pack_at[v]
        low = at & 127
        value = None
        for u in SLOT_TILES[v]:
            got = lanes(rows[u], low)
            value = got if value is None else jnp.where((at >> 7) == u, got, value)
        return value

    def second_copy(k, r):
        low, size = GROUPS[k]
        peer = (me_l + r) % NL
        return pltpu.make_async_remote_copy(
            src_ref=m_buf.at[peer, pl.ds(low, size)],
            dst_ref=r_buf.at[pl.ds(low, size), me_l],
            send_sem=second_send.at[k],
            recv_sem=second_recv.at[k],
            device_id={"comp": me_c, "lat": peer},
            device_id_type=pl.DeviceIdType.MESH,
        )

    def second_local(k):
        low, size = GROUPS[k]
        return pltpu.make_async_copy(
            m_buf.at[me_l, pl.ds(low, size)], r_buf.at[pl.ds(low, size), me_l], second_own.at[k]
        )

    def many(ref, k, sem):
        low, size = GROUPS[k]
        part = ref.at[pl.ds(low, size), pl.ds(0, NL - 1)]
        return pltpu.make_async_copy(part, part, sem.at[k])

    def pack_tile(tile, carry):
        rows = [a_rows(FOLD * tile + s) for s in range(FOLD)]
        octet = jnp.minimum(tile, 2) * 8
        for v in range(TILES):
            parts = [windows(FOLD * tile + s, v, rows[s]) for s in range(FOLD)]
            spare = w_last[v]
            for b, value in enumerate(swap_blocks(parts, block_masks, turns)):
                if FOLD * v + b < NL:
                    extra = lanes(spare, BUCKET * b + octet + (lane & 7))
                    m_buf[FOLD * v + b, tile] = jnp.where(lane >= 120, extra, value)
        return carry

    def arrived(g):
        first_wait(g, first_recv).wait()
        first_local(g).wait()

    arrived(0)
    rows = a_rows(LAST)
    for v in range(TILES):
        w_last[v] = windows(LAST, v, rows)
    waited = 1
    for k, (low, size) in enumerate(GROUPS):
        need = min(FOLD * (low + size) - 1, 31) // 8 + 1
        while waited <= need:
            arrived(waited)
            waited += 1
        lax.fori_loop(low, low + size, pack_tile, 0)

        def send(r, carry, k=k):
            second_copy(k, r).start()
            return carry

        lax.fori_loop(1, NL, send, 0)
        second_local(k).start()

    r_rows = r_buf.reshape(TILES, NL * 8, 128)

    def turn_in(tile, carry):
        for h in range(2):
            p_buf[tile, h] = r_rows[tile, pl.ds(h, 128, stride=2), :].T
        return carry

    for k, (low, size) in enumerate(GROUPS):
        many(r_buf, k, second_recv).wait()
        second_local(k).wait()
        lax.fori_loop(low, low + size, turn_in, 0)

    def point_rows(tile, s, u, h):
        if s is None:
            return p_buf[u, h, 120:128, :]
        return p_buf[tile, h, BUCKET * s + 8 * u : BUCKET * s + 8 * u + 8, :]

    def place(direction, tile, s):
        held = {(u, h): point_rows(tile, s, u, h) for u in range(3) for h in range(2)}
        cosine = trig[0, direction]
        sign = jnp.where(cosine >= 0.0, 1, -1)
        for v in range(ROWS):
            index = row_at[v]
            which = row_tile[v]
            value = None
            for u in POINT_TILES[v]:
                for h in range(2):
                    got = sublanes(held[u, h], index)
                    value = got if value is None else jnp.where(which == 2 * u + h, got, value)
            q = jnp.where(msk[pl.ds(8 * v, 8), :] > 0.0, lanes(value, lane_at[v]), 0.0)
            x_ext[0, direction, v + 2] = sweep_x(q, cosine * sx[v], sign, sub, lane)

    def place_tile(tile, carry):
        for s in range(FOLD):
            place(FOLD * tile + s, tile, s)
        return carry

    lax.fori_loop(0, TILES, place_tile, 0)
    place(LAST, None, None)

    def halo_copy(step, k):
        positive = pl.ds(0, SIN_POS)
        negative = pl.ds(SIN_POS, ND - SIN_POS)
        which, source_rows, target_rows, peer = (
            (positive, pl.ds(8, 2), pl.ds(0, 2), north),
            (negative, pl.ds(9, 1), pl.ds(1, 1), north),
            (positive, pl.ds(2, 1), pl.ds(10, 1), south),
            (negative, pl.ds(2, 2), pl.ds(10, 2), south),
        )[k]
        return pltpu.make_async_remote_copy(
            src_ref=x_ext.at[step, which, source_rows],
            dst_ref=x_ext.at[step, which, target_rows],
            send_sem=halo_send.at[step, k],
            recv_sem=halo_recv.at[step, k],
            device_id=peer,
            device_id_type=pl.DeviceIdType.MESH,
        )

    def sweep_y(step, positive, row_list):
        def body(direction, carry):
            sine = trig[1, direction]

            def row(r):
                value = x_ext[step, direction, r + 2]
                if r < 0:
                    value = jnp.where(me_l > 0, value, 0.0)
                if r >= ROWS:
                    value = jnp.where(me_l < NL - 1, value, 0.0)
                return value

            diffs = {}
            fluxes = {}

            def diff(f):
                if f not in diffs:
                    diffs[f] = row(f) - row(f - 1)
                return diffs[f]

            def face(f):
                if f not in fluxes:
                    if positive:
                        curvature = diff(f) - diff(f - 1)
                    else:
                        curvature = diff(f + 1) - diff(f)
                    fluxes[f] = flux(row(f - 1), diff(f), curvature, sine * sy[f])
                return fluxes[f]

            for r in row_list:
                y_buf[direction, r] = row(r) - (face(r + 1) - face(r))
            return carry

        if positive:
            lax.fori_loop(0, SIN_POS, body, 0)
        else:
            lax.fori_loop(SIN_POS, ND, body, 0)

    def sweep_theta(step, r):
        t = trn[pl.ds(pl.multiple_of(8 * r, 8), 8), :]
        forward = t >= 0.0
        q = [y_buf[j, r] for j in range(ND)]
        d = [q[(j + 1) % ND] - q[j] for j in range(ND)]

        def face(j):
            ahead = d[(j + 1) % ND] - d[j]
            behind = d[j] - d[j - 1]
            if TURN[j] >= 0:
                curvature = jnp.where(forward, behind, ahead)
            else:
                curvature = jnp.where(forward, ahead, behind)
            return flux(q[j], d[j], curvature, float(TURN[j]) * t)

        last = face(ND - 1)
        prior = last
        for j in range(ND):
            f = last if j == ND - 1 else face(j)
            value = q[j] - (f - prior)
            prior = f
            if step == 0:
                sign = 1 if COS[j] >= 0 else -1
                x_ext[1, j, r + 2] = sweep_x(value, float(COS[j]) * sx[r], sign, sub, lane)
            else:
                y_buf[j, r] = value

    inner = tuple(range(2, 6))
    outer = (0, 1, 6, 7)
    for step in range(2):
        for k in range(4):
            halo_copy(step, k).start()
        sweep_y(step, True, inner)
        sweep_y(step, False, inner)

        def inner_rows(r, carry, step=step):
            sweep_theta(step, r)
            return carry

        def outer_rows(k, carry, step=step):
            sweep_theta(step, k + 4 * (k // 2))
            return carry

        lax.fori_loop(2, 6, inner_rows, 0)
        for k in range(4):
            halo_copy(step, k).wait()
        sweep_y(step, True, outer)
        sweep_y(step, False, outer)
        lax.fori_loop(0, 4, outer_rows, 0)

    def collect(direction, tile, s):
        taken = [lanes(y_buf[direction, v], take_at[v]) for v in range(ROWS)]
        for u in range(3):
            for h in range(2):
                index = back_row[u, h]
                which = back_tile[u, h]
                value = None
                for v in ROW_TILES[u]:
                    got = sublanes(taken[v], index)
                    value = got if value is None else jnp.where(which == v, got, value)
                if s is None:
                    p_buf[u, h, 120:128, :] = value
                else:
                    p_buf[tile, h, BUCKET * s + 8 * u : BUCKET * s + 8 * u + 8, :] = value

    def third_copy(k, r):
        low, size = GROUPS[k]
        peer = (me_l + r) % NL
        return pltpu.make_async_remote_copy(
            src_ref=m_buf.at[peer, pl.ds(low, size)],
            dst_ref=n_buf.at[pl.ds(low, size), me_l],
            send_sem=third_send.at[k],
            recv_sem=third_recv.at[k],
            device_id={"comp": me_c, "lat": peer},
            device_id_type=pl.DeviceIdType.MESH,
        )

    def third_local(k):
        low, size = GROUPS[k]
        return pltpu.make_async_copy(
            m_buf.at[me_l, pl.ds(low, size)], n_buf.at[pl.ds(low, size), me_l], third_own.at[k]
        )

    for k in range(len(GROUPS)):
        many(r_buf, k, second_send).wait()

    m_rows = m_buf.reshape(NL * TILES * 8, 128)

    def turn_out(tile, carry):
        for h in range(2):
            r_rows[tile, pl.ds(h, 128, stride=2), :] = p_buf[tile, h].T
        for l in range(NL):
            m_buf[l, tile] = r_buf[tile, l]
        return carry

    def collect_tile(tile, carry):
        for s in range(FOLD):
            collect(FOLD * tile + s, tile, s)
        turn_out(tile, 0)
        return carry

    collect(LAST, None, None)
    for k, (low, size) in enumerate(GROUPS):
        lax.fori_loop(low, low + size, collect_tile, 0)

        def send(r, carry, k=k):
            third_copy(k, r).start()
            return carry

        lax.fori_loop(1, NL, send, 0)
        third_local(k).start()

    def put(direction, parts):
        for u in range(6):
            at = put_at[u]
            which = put_tile[u]
            value = jnp.zeros((8, 128), jnp.float32)
            for v in range(TILES):
                if u in SLOT_TILES[v]:
                    value = jnp.where(which == v, lanes(parts[v], at), value)
            o_buf[direction, :, pl.ds(128 * u, 128)] = value

    def put_tile_of(tile, carry):
        swapped = []
        for v in range(TILES):
            parts = [n_buf[tile, min(FOLD * v + b, NL - 1)] for b in range(FOLD)]
            swapped.append(swap_blocks(parts, block_masks, turns))
        for s in range(FOLD):
            put(FOLD * tile + s, [swapped[v][s] for v in range(TILES)])
        return carry

    def put_last():
        parts = []
        spare = 120 + (lane & 7)
        for v in range(TILES):
            value = jnp.zeros((8, 128), jnp.float32)
            for b in range(FOLD):
                if FOLD * v + b < NL:
                    for e in range(3):
                        got = lanes(n_buf[e, FOLD * v + b], spare)
                        value = jnp.where((lane >> 3) == 3 * b + e, got, value)
            parts.append(value)
        put(LAST, parts)

    def fourth_ends(k, peer):
        part = pl.ds(*PIECES[k])
        return o_buf.at[part, slot_of(peer), :], out.at[part, me_c, :]

    def fourth_copy(k, r):
        peer = (me_c + r) % NC
        source_ref, target_ref = fourth_ends(k, peer)
        return pltpu.make_async_remote_copy(
            src_ref=source_ref,
            dst_ref=target_ref,
            send_sem=fourth_send.at[k],
            recv_sem=fourth_recv.at[k],
            device_id={"comp": peer, "lat": me_l},
            device_id_type=pl.DeviceIdType.MESH,
        )

    def fourth_local(k):
        source_ref, target_ref = fourth_ends(k, me_c)
        return pltpu.make_async_copy(source_ref, target_ref, fourth_own.at[k])

    for k, (low, size) in enumerate(GROUPS):
        many(n_buf, k, third_recv).wait()
        third_local(k).wait()
        lax.fori_loop(low, low + size, put_tile_of, 0)
    put_last()
    for k in range(len(PIECES)):
        for r in range(1, NC):
            fourth_copy(k, r).start()
        fourth_local(k).start()

    for g in range(len(CHUNKS)):
        first_wait(g, first_send).wait()
    for k in range(len(GROUPS)):
        many(n_buf, k, third_send).wait()
    for k, (low, size) in enumerate(PIECES):
        fourth_local(k).wait()
        part = out.at[pl.ds(low, size), pl.ds(0, NC - 1), :]
        pltpu.make_async_copy(part, part, fourth_recv.at[k]).wait()
        pltpu.make_async_copy(part, part, fourth_send.at[k]).wait()


def per_device(spectra_in, group_speed, turn_rate, sea_mask, sea_cell, slab_counts):
    f32 = jnp.float32
    vreg = (8, 128)
    dma = pltpu.SemaphoreType.DMA
    vmem = pl.BlockSpec(memory_space=pltpu.VMEM)
    smem = pl.BlockSpec(memory_space=pltpu.SMEM)
    anywhere = pl.BlockSpec(memory_space=pl.ANY)
    chunks, groups, pieces = len(CHUNKS), len(GROUPS), len(PIECES)
    return pl.pallas_call(
        kernel,
        out_shape=jax.ShapeDtypeStruct((ND, NC, SLOTS), f32),
        in_specs=[anywhere, vmem, vmem, vmem, vmem, smem, smem],
        out_specs=anywhere,
        scratch_shapes=[
            pltpu.VMEM((ND, NC, SLOTS), f32),
            pltpu.VMEM((NL, TILES) + vreg, f32),
            pltpu.VMEM((TILES, NL) + vreg, f32),
            pltpu.VMEM((TILES, 2, 128, 128), f32),
            pltpu.VMEM((TILES, NL) + vreg, f32),
            pltpu.VMEM((ND, NC, SLOTS), f32),
            pltpu.VMEM((2, ND, ROWS + 4) + vreg, f32),
            pltpu.VMEM((ND, ROWS) + vreg, f32),
            pltpu.VMEM((64, 128), f32),
            pltpu.VMEM((64, 128), f32),
            pltpu.VMEM((64, 128), f32),
            pltpu.VMEM((4,) + vreg, f32),
            pltpu.VMEM((ROWS,) + vreg, f32),
            pltpu.VMEM((ROWS + 1,) + vreg, f32),
            pltpu.VMEM((TILES,) + vreg, jnp.int32),
            pltpu.VMEM((6,) + vreg, jnp.int32),
            pltpu.VMEM((6,) + vreg, jnp.int32),
            pltpu.VMEM((ROWS,) + vreg, jnp.int32),
            pltpu.VMEM((ROWS,) + vreg, jnp.int32),
            pltpu.VMEM((ROWS,) + vreg, jnp.int32),
            pltpu.VMEM((ROWS,) + vreg, jnp.int32),
            pltpu.VMEM((3, 2) + vreg, jnp.int32),
            pltpu.VMEM((3, 2) + vreg, jnp.int32),
            pltpu.VMEM((TILES,) + vreg, f32),
            dma((chunks,)), dma((chunks,)), dma((chunks,)),
            dma((groups,)), dma((groups,)), dma((groups,)),
            dma((4,)), dma((4,)), dma((2, 4)), dma((2, 4)),
            dma((groups,)), dma((groups,)), dma((groups,)),
            dma((pieces,)), dma((pieces,)), dma((pieces,)),
        ],
        compiler_params=pltpu.CompilerParams(
            collective_id=0, has_side_effects=True, vmem_limit_bytes=40 * 1024 * 1024
        ),
        name="wave_step",
    )(
        spectra_in.transpose(1, 0, 2),
        group_speed,
        turn_rate,
        sea_mask,
        sea_cell.reshape(48, 128),
        slab_counts,
        jnp.asarray(np.stack([COS, SIN])),
    ).transpose(1, 0, 2)


def solution(mesh):
    in_specs = (
        P(None, None, ("comp", "lat")),
        P("comp", "lat", None),
        P("comp", "lat", None),
        P("lat", None),
        P("lat"),
        P(),
    )
    out_specs = P(None, None, ("comp", "lat"))
    return jax.shard_map(
        per_device, mesh=mesh, in_specs=in_specs, out_specs=out_specs, check_vma=False
    )
```

time: 398 us -> 109 us (0.27); the launches traced: 391 us -> 109 us
  local copies, waits for them, and re-layouts: 128 us -> 5.77 us
  Pallas kernels: 0 us -> 103 us
  blocking collectives: 59.9 us -> 0 us
  other arithmetic: 58.5 us -> 0 us
  matrix products: 43.5 us -> 0 us
  waiting for transfers between devices: 33.2 us -> 0 us
  starting transfers between devices: 32.9 us -> 0 us
  loops' own time: 32.2 us -> 0 us
    pallas_call x0 -> x1, Pallas kernels: none -> 103 us  [per_device(): pl.pallas_call(kernel, out_shape=jax.ShapeDtypeStruct((ND, NC, SLOTS), f3...]
    all_to_all x2 -> x0, blocking collectives: 59.9 us -> none  [the longest x1 36.1 us: per_device(): lax.all_to_all(values, 'lat', split_axis=3, concat_axis=3, tiled=True)]
    unnamed x67 -> x15, local copies, waits for them, and re-layouts: 51.2 us -> 5.77 us
    dot_general x18 -> x0, matrix products: 43.5 us -> none  [the longest x8 17.7 us: take_row(): jnp.einsum('fdc,pc->fdp', grid_row, matrix, precision=highest, preferred_...]
    another operation x2 -> x0, loops' own time: 32.2 us -> none  [the longest x1 16.3 us: per_device(): lax.fori_loop(0, row_count, place_row, jnp.zeros((freq_own, dir_count, ce...]
    dynamic_slice x43 -> x0, local copies, waits for them, and re-layouts: 27.9 us -> none  [the longest x16 12.5 us: row_matrix(): window_cells = lax.dynamic_slice_in_dim(cell_padded, offset, columns)]
    dynamic_update_slice x9 -> x0, local copies, waits for them, and re-layouts: 24.1 us -> none  [the longest x8 12.2 us: take_row(): lax.dynamic_update_slice_in_dim(collected, current + portion, offset, axi...]
    all_to_all x2 -> x0, waiting for transfers between devices: 20.9 us -> none  [the longest x1 12.9 us: per_device(): lax.all_to_all(lax.all_to_all(packed, 'comp', split_axis=0, concat_axis=2...]
  transfers between devices with their start and end apart: 8 -> 0, of which waited for: 6 -> 0; matrix products, arithmetic and copies ran while one was open for 7% -> 0% of each run, Pallas kernels for 0% -> 0%
where the time goes in v1:
time: 109 us
  Pallas kernels  103 us (94%)
  local copies, waits for them, and re-layouts  5.77 us (5%)
    pallas_call x1, Pallas kernels, per_device(): pl.pallas_call(kernel, out_shape=jax.ShapeDtypeStruct((ND, NC, SLOTS), f3...  103 us
    unnamed x15, local copies, waits for them, and re-layouts  5.77 us

profile of v1, /device:TPU:1, one launch (start us, length us, event | category | flops | bytes accessed | tf_op | source)
XLA Modules:
  0.0 108.6 jit_solution(16731890456773675388)
XLA Ops:
  0.0 0.0 copy-start.5
  0.0 0.0 copy-start.6
  0.0 0.7 copy-done.5
  0.7 0.0 copy-done.6
  0.7 0.0 copy-start
  0.7 1.2 %copy-done = f32[8,36,768]{2,0,1:T(8,128)S(1)} copy-done((f32[8,36,768]{2,0,1:T(8,128)S(1)}, f32[8,36,768]{2,0,1:T(8,128)}, u32[]{:S(2)}) %copy-start) | copy-done | bytes 884760
  1.9 0.0 copy-start.1
  1.9 0.8 copy-done.1
  2.6 0.0 copy-start.2
  2.6 0.8 copy-done.2
  3.4 0.0 copy-start.3
  3.4 0.8 copy-done.3
  4.1 0.0 copy-start.4
  4.1 0.7 copy-done.4
  4.9 102.8 %wave_step.1 = f32[36,8,768]{2,1,0:T(8,128)S(1)} custom-call(f32[36,8,768]{2,1,0:T(8,128)S(1)} %bitcast.4, f32[1,8,1024]{2,1,0:T(8,128)S(1)} %copy-done.1, f32[1,8,1024]{2,1,0:T(8,128)S(1)} %copy-done.2, s32[8,1024]{1,0:T(8,128)S(1)} %copy-done.3, s32[48,128]{1,0:T(8,128)S(1)} %bitcast.5, s32[32]{0:T(128)S(1)} %copy-done.6, f32[2,36]{1,0:T(2,128)S(1)} %copy-done.5), custom_call_target="tpu_custom_call" | custom-call | tf_op jit(solution)/shard_map/wave_step/pallas_call | solution.py:635
  107.7 0.9 copy.9
Async XLA Ops:
  0.0 0.7 copy-start.5
  0.0 0.7 copy-start.6
  0.7 1.2 %copy-start = (f32[8,36,768]{2,0,1:T(8,128)S(1)}, f32[8,36,768]{2,0,1:T(8,128)}, u32[]{:S(2)}) copy-start(f32[8,36,768]{2,0,1:T(8,128)} %param.7) | copy-start | bytes 2654212
  1.9 0.8 copy-start.1
  2.6 0.8 copy-start.2
  3.4 0.8 copy-start.3
  4.1 0.7 copy-start.4

commit v2 on v1

--- a/solution.py
+++ b/solution.py
@@ -17,9 +17,6 @@
 FOLD = 5
 TILES = 7
 LAST = ND - 1
-CHUNKS = ((32, 4), (0, 8), (8, 8), (16, 8), (24, 8))
-GROUPS = ((0, 2), (2, 2), (4, 3))
-PIECES = ((0, 32), (32, 4))
 SIN_POS = 19
 
 ANGLES = np.arange(ND, dtype=np.float32) * np.float32(2.0 * math.pi / ND)
@@ -88,7 +85,8 @@
 
 
 def kernel(
-    spectra, speed, turn, mask, cells, counts, trig, out,
+    spectra, speed_in, turn_in, mask_in, cells_in, counts_in, out,
+    speed, turn, mask, cells, counts, trig, load_sem,
     a_buf, m_buf, r_buf, p_buf, n_buf, o_buf, x_ext, y_buf,
     spd, trn, msk, stat_halo, sx, sy,
     pack_at, put_at, put_tile, row_at, row_tile, lane_at, take_at, back_row, back_tile, w_last,
@@ -103,15 +101,26 @@
     def slot_of(c):
         return (c % 4) * 2 + c // 4
 
+    loads = [
+        pltpu.make_async_copy(source_ref, target_ref, load_sem.at[k])
+        for k, (source_ref, target_ref) in enumerate(
+            ((counts_in, counts), (speed_in, speed), (turn_in, turn), (mask_in, mask), (cells_in, cells))
+        )
+    ]
+    for load in loads:
+        load.start()
+
+    def chunk(g):
+        return pl.ds(FOLD * g, 1 if isinstance(g, int) and g == TILES else FOLD)
+
     def first_ends(g, peer):
-        part = pl.ds(*CHUNKS[g])
-        return spectra.at[part, peer, :], a_buf.at[part, slot_of(me_c), :]
+        return spectra.at[chunk(g), peer, :], a_buf.at[chunk(g), slot_of(me_c), :]
 
     def first_local(g):
         source_ref, target_ref = first_ends(g, me_c)
         return pltpu.make_async_copy(source_ref, target_ref, first_own.at[g])
 
-    for g in range(len(CHUNKS)):
+    for g in range(TILES + 1):
         first_local(g).start()
 
     barrier = pltpu.get_barrier_semaphore()
@@ -131,6 +140,12 @@
     lax.fori_loop(1, NC, greet_comp, 0)
     lax.fori_loop(1, NL, greet_lat, 0)
 
+    for j in range(ND):
+        trig[0, j] = jnp.float32(float(COS[j]))
+        trig[1, j] = jnp.float32(float(SIN[j]))
+
+    for load in loads:
+        load.wait()
     starts = [jnp.int32(0)]
     for slab in range(NL):
         starts.append(starts[-1] + counts[slab])
@@ -158,47 +173,6 @@
         spd[pl.ds(t, 8, stride=8), :] = speed[0, :, columns]
         trn[pl.ds(t, 8, stride=8), :] = turn[0, :, columns]
         msk[pl.ds(t, 8, stride=8), :] = mask[:, columns].astype(jnp.float32)
-
-    pl.semaphore_wait(barrier, NC - 1 + NL - 1)
-
-    def first_copy(g, r):
-        peer = (me_c + r) % NC
-        source_ref, target_ref = first_ends(g, peer)
-        return pltpu.make_async_remote_copy(
-            src_ref=source_ref,
-            dst_ref=target_ref,
-            send_sem=first_send.at[g],
-            recv_sem=first_recv.at[g],
-            device_id={"comp": peer, "lat": me_l},
-            device_id_type=pl.DeviceIdType.MESH,
-        )
-
-    for g in range(len(CHUNKS)):
-        for r in range(1, NC):
-            first_copy(g, r).start()
-
-    north = {"comp": me_c, "lat": (me_l + 1) % NL}
-    south = {"comp": me_c, "lat": (me_l + NL - 1) % NL}
-
-    def stat_copy(k):
-        ref = (spd, msk)[k % 2]
-        row = 56 if k < 2 else 0
-        return pltpu.make_async_remote_copy(
-            src_ref=ref.at[pl.ds(row, 8), :],
-            dst_ref=stat_halo.at[k],
-            send_sem=stat_send.at[k],
-            recv_sem=stat_recv.at[k],
-            device_id=north if k < 2 else south,
-            device_id_type=pl.DeviceIdType.MESH,
-        )
-
-    for k in range(4):
-        stat_copy(k).start()
-
-    def first_wait(g, sem):
-        low, size = CHUNKS[g]
-        ref = a_buf.at[pl.ds(low, size), pl.ds(0, NC - 1), :]
-        return pltpu.make_async_copy(ref, ref, sem.at[g])
 
     for u in range(6):
         point = source + (lane + 128 * u) * 256
@@ -266,6 +240,46 @@
         if v < ROWS - 1:
             after = pl.ds(8 * v + 8, 8)
             sy[v + 1] = 0.5 * (s + spd[after, :]) * m * msk[after, :]
+    pl.semaphore_wait(barrier, NC - 1 + NL - 1)
+
+    def first_wait(g, sem):
+        ref = a_buf.at[chunk(g), pl.ds(0, NC - 1), :]
+        return pltpu.make_async_copy(ref, ref, sem.at[g])
+
+    def first_copy(g, r):
+        peer = (me_c + r) % NC
+        source_ref, target_ref = first_ends(g, peer)
+        return pltpu.make_async_remote_copy(
+            src_ref=source_ref,
+            dst_ref=target_ref,
+            send_sem=first_send.at[g],
+            recv_sem=first_recv.at[g],
+            device_id={"comp": peer, "lat": me_l},
+            device_id_type=pl.DeviceIdType.MESH,
+        )
+
+    for g in (TILES,) + tuple(range(TILES)):
+        for r in range(1, NC):
+            first_copy(g, r).start()
+
+    north = {"comp": me_c, "lat": (me_l + 1) % NL}
+    south = {"comp": me_c, "lat": (me_l + NL - 1) % NL}
+
+    def stat_copy(k):
+        ref = (spd, msk)[k % 2]
+        row = 56 if k < 2 else 0
+        return pltpu.make_async_remote_copy(
+            src_ref=ref.at[pl.ds(row, 8), :],
+            dst_ref=stat_halo.at[k],
+            send_sem=stat_send.at[k],
+            recv_sem=stat_recv.at[k],
+            device_id=north if k < 2 else south,
+            device_id_type=pl.DeviceIdType.MESH,
+        )
+
+    for k in range(4):
+        stat_copy(k).start()
+
     for k in range(4):
         stat_copy(k).wait()
     south_mask = jnp.where(me_l > 0, stat_halo[1], 0.0)
@@ -285,30 +299,26 @@
             value = got if value is None else jnp.where((at >> 7) == u, got, value)
         return value
 
-    def second_copy(k, r):
-        low, size = GROUPS[k]
+    def second_copy(tile, r):
         peer = (me_l + r) % NL
         return pltpu.make_async_remote_copy(
-            src_ref=m_buf.at[peer, pl.ds(low, size)],
-            dst_ref=r_buf.at[pl.ds(low, size), me_l],
-            send_sem=second_send.at[k],
-            recv_sem=second_recv.at[k],
+            src_ref=m_buf.at[peer, tile],
+            dst_ref=r_buf.at[tile, me_l],
+            send_sem=second_send.at[tile],
+            recv_sem=second_recv.at[tile],
             device_id={"comp": me_c, "lat": peer},
             device_id_type=pl.DeviceIdType.MESH,
         )
 
-    def second_local(k):
-        low, size = GROUPS[k]
-        return pltpu.make_async_copy(
-            m_buf.at[me_l, pl.ds(low, size)], r_buf.at[pl.ds(low, size), me_l], second_own.at[k]
-        )
-
-    def many(ref, k, sem):
-        low, size = GROUPS[k]
-        part = ref.at[pl.ds(low, size), pl.ds(0, NL - 1)]
-        return pltpu.make_async_copy(part, part, sem.at[k])
+    def second_local(tile):
+        return pltpu.make_async_copy(m_buf.at[me_l, tile], r_buf.at[tile, me_l], second_own.at[tile])
+
+    def many(ref, tile, sem):
+        part = ref.at[tile, pl.ds(0, NL - 1)]
+        return pltpu.make_async_copy(part, part, sem.at[tile])
 
     def pack_tile(tile, carry):
+        arrived(tile)
         rows = [a_rows(FOLD * tile + s) for s in range(FOLD)]
         octet = jnp.minimum(tile, 2) * 8
         for v in range(TILES):
@@ -318,42 +328,31 @@
                 if FOLD * v + b < NL:
                     extra = lanes(spare, BUCKET * b + octet + (lane & 7))
                     m_buf[FOLD * v + b, tile] = jnp.where(lane >= 120, extra, value)
+        for r in range(1, NL):
+            second_copy(tile, r).start()
+        second_local(tile).start()
         return carry
 
     def arrived(g):
         first_wait(g, first_recv).wait()
         first_local(g).wait()
 
-    arrived(0)
+    arrived(TILES)
     rows = a_rows(LAST)
     for v in range(TILES):
         w_last[v] = windows(LAST, v, rows)
-    waited = 1
-    for k, (low, size) in enumerate(GROUPS):
-        need = min(FOLD * (low + size) - 1, 31) // 8 + 1
-        while waited <= need:
-            arrived(waited)
-            waited += 1
-        lax.fori_loop(low, low + size, pack_tile, 0)
-
-        def send(r, carry, k=k):
-            second_copy(k, r).start()
-            return carry
-
-        lax.fori_loop(1, NL, send, 0)
-        second_local(k).start()
+    lax.fori_loop(0, TILES, pack_tile, 0)
 
     r_rows = r_buf.reshape(TILES, NL * 8, 128)
 
-    def turn_in(tile, carry):
+    def turn_points(tile, carry):
+        many(r_buf, tile, second_recv).wait()
+        second_local(tile).wait()
         for h in range(2):
             p_buf[tile, h] = r_rows[tile, pl.ds(h, 128, stride=2), :].T
         return carry
 
-    for k, (low, size) in enumerate(GROUPS):
-        many(r_buf, k, second_recv).wait()
-        second_local(k).wait()
-        lax.fori_loop(low, low + size, turn_in, 0)
+    lax.fori_loop(0, TILES, turn_points, 0)
 
     def point_rows(tile, s, u, h):
         if s is None:
@@ -504,28 +503,22 @@
                 else:
                     p_buf[tile, h, BUCKET * s + 8 * u : BUCKET * s + 8 * u + 8, :] = value
 
-    def third_copy(k, r):
-        low, size = GROUPS[k]
+    def third_copy(tile, r):
         peer = (me_l + r) % NL
         return pltpu.make_async_remote_copy(
-            src_ref=m_buf.at[peer, pl.ds(low, size)],
-            dst_ref=n_buf.at[pl.ds(low, size), me_l],
-            send_sem=third_send.at[k],
-            recv_sem=third_recv.at[k],
+            src_ref=m_buf.at[peer, tile],
+            dst_ref=n_buf.at[tile, me_l],
+            send_sem=third_send.at[tile],
+            recv_sem=third_recv.at[tile],
             device_id={"comp": me_c, "lat": peer},
             device_id_type=pl.DeviceIdType.MESH,
         )
 
-    def third_local(k):
-        low, size = GROUPS[k]
-        return pltpu.make_async_copy(
-            m_buf.at[me_l, pl.ds(low, size)], n_buf.at[pl.ds(low, size), me_l], third_own.at[k]
-        )
-
-    for k in range(len(GROUPS)):
-        many(r_buf, k, second_send).wait()
-
-    m_rows = m_buf.reshape(NL * TILES * 8, 128)
+    def third_local(tile):
+        return pltpu.make_async_copy(m_buf.at[me_l, tile], n_buf.at[tile, me_l], third_own.at[tile])
+
+    for tile in range(TILES):
+        many(r_buf, tile, second_send).wait()
 
     def turn_out(tile, carry):
         for h in range(2):
@@ -538,18 +531,13 @@
         for s in range(FOLD):
             collect(FOLD * tile + s, tile, s)
         turn_out(tile, 0)
+        for r in range(1, NL):
+            third_copy(tile, r).start()
+        third_local(tile).start()
         return carry
 
     collect(LAST, None, None)
-    for k, (low, size) in enumerate(GROUPS):
-        lax.fori_loop(low, low + size, collect_tile, 0)
-
-        def send(r, carry, k=k):
-            third_copy(k, r).start()
-            return carry
-
-        lax.fori_loop(1, NL, send, 0)
-        third_local(k).start()
+    lax.fori_loop(0, TILES, collect_tile, 0)
 
     def put(direction, parts):
         for u in range(6):
@@ -561,13 +549,41 @@
                     value = jnp.where(which == v, lanes(parts[v], at), value)
             o_buf[direction, :, pl.ds(128 * u, 128)] = value
 
+    def fourth_ends(k, peer):
+        part = chunk(k)
+        return o_buf.at[part, slot_of(peer), :], out.at[part, me_c, :]
+
+    def fourth_copy(k, r):
+        peer = (me_c + r) % NC
+        source_ref, target_ref = fourth_ends(k, peer)
+        return pltpu.make_async_remote_copy(
+            src_ref=source_ref,
+            dst_ref=target_ref,
+            send_sem=fourth_send.at[k],
+            recv_sem=fourth_recv.at[k],
+            device_id={"comp": peer, "lat": me_l},
+            device_id_type=pl.DeviceIdType.MESH,
+        )
+
+    def fourth_local(k):
+        source_ref, target_ref = fourth_ends(k, me_c)
+        return pltpu.make_async_copy(source_ref, target_ref, fourth_own.at[k])
+
+    def fourth_send_all(k):
+        for r in range(1, NC):
+            fourth_copy(k, r).start()
+        fourth_local(k).start()
+
     def put_tile_of(tile, carry):
+        many(n_buf, tile, third_recv).wait()
+        third_local(tile).wait()
         swapped = []
         for v in range(TILES):
             parts = [n_buf[tile, min(FOLD * v + b, NL - 1)] for b in range(FOLD)]
             swapped.append(swap_blocks(parts, block_masks, turns))
         for s in range(FOLD):
             put(FOLD * tile + s, [swapped[v][s] for v in range(TILES)])
+        fourth_send_all(tile)
         return carry
 
     def put_last():
@@ -583,43 +599,18 @@
             parts.append(value)
         put(LAST, parts)
 
-    def fourth_ends(k, peer):
-        part = pl.ds(*PIECES[k])
-        return o_buf.at[part, slot_of(peer), :], out.at[part, me_c, :]
-
-    def fourth_copy(k, r):
-        peer = (me_c + r) % NC
-        source_ref, target_ref = fourth_ends(k, peer)
-        return pltpu.make_async_remote_copy(
-            src_ref=source_ref,
-            dst_ref=target_ref,
-            send_sem=fourth_send.at[k],
-            recv_sem=fourth_recv.at[k],
-            device_id={"comp": peer, "lat": me_l},
-            device_id_type=pl.DeviceIdType.MESH,
-        )
-
-    def fourth_local(k):
-        source_ref, target_ref = fourth_ends(k, me_c)
-        return pltpu.make_async_copy(source_ref, target_ref, fourth_own.at[k])
-
-    for k, (low, size) in enumerate(GROUPS):
-        many(n_buf, k, third_recv).wait()
-        third_local(k).wait()
-        lax.fori_loop(low, low + size, put_tile_of, 0)
+    lax.fori_loop(0, 3, put_tile_of, 0)
     put_last()
-    for k in range(len(PIECES)):
-        for r in range(1, NC):
-            fourth_copy(k, r).start()
-        fourth_local(k).start()
-
-    for g in range(len(CHUNKS)):
+    fourth_send_all(TILES)
+    lax.fori_loop(3, TILES, put_tile_of, 0)
+
+    for g in range(TILES + 1):
         first_wait(g, first_send).wait()
-    for k in range(len(GROUPS)):
-        many(n_buf, k, third_send).wait()
-    for k, (low, size) in enumerate(PIECES):
+    for tile in range(TILES):
+        many(n_buf, tile, third_send).wait()
+    for k in range(TILES + 1):
         fourth_local(k).wait()
-        part = out.at[pl.ds(low, size), pl.ds(0, NC - 1), :]
+        part = out.at[chunk(k), pl.ds(0, NC - 1), :]
         pltpu.make_async_copy(part, part, fourth_recv.at[k]).wait()
         pltpu.make_async_copy(part, part, fourth_send.at[k]).wait()
 
@@ -628,16 +619,21 @@
     f32 = jnp.float32
     vreg = (8, 128)
     dma = pltpu.SemaphoreType.DMA
-    vmem = pl.BlockSpec(memory_space=pltpu.VMEM)
-    smem = pl.BlockSpec(memory_space=pltpu.SMEM)
+    hbm = pl.BlockSpec(memory_space=pltpu.HBM)
     anywhere = pl.BlockSpec(memory_space=pl.ANY)
-    chunks, groups, pieces = len(CHUNKS), len(GROUPS), len(PIECES)
     return pl.pallas_call(
         kernel,
         out_shape=jax.ShapeDtypeStruct((ND, NC, SLOTS), f32),
-        in_specs=[anywhere, vmem, vmem, vmem, vmem, smem, smem],
+        in_specs=[hbm] * 6,
         out_specs=anywhere,
         scratch_shapes=[
+            pltpu.VMEM((1, ROWS, 1024), f32),
+            pltpu.VMEM((1, ROWS, 1024), f32),
+            pltpu.VMEM((ROWS, 1024), jnp.int32),
+            pltpu.VMEM((48, 128), jnp.int32),
+            pltpu.SMEM((NL,), jnp.int32),
+            pltpu.SMEM((2, ND), f32),
+            dma((5,)),
             pltpu.VMEM((ND, NC, SLOTS), f32),
             pltpu.VMEM((NL, TILES) + vreg, f32),
             pltpu.VMEM((TILES, NL) + vreg, f32),
@@ -662,14 +658,14 @@
             pltpu.VMEM((3, 2) + vreg, jnp.int32),
             pltpu.VMEM((3, 2) + vreg, jnp.int32),
             pltpu.VMEM((TILES,) + vreg, f32),
-            dma((chunks,)), dma((chunks,)), dma((chunks,)),
-            dma((groups,)), dma((groups,)), dma((groups,)),
+            dma((TILES + 1,)), dma((TILES + 1,)), dma((TILES + 1,)),
+            dma((TILES,)), dma((TILES,)), dma((TILES,)),
             dma((4,)), dma((4,)), dma((2, 4)), dma((2, 4)),
-            dma((groups,)), dma((groups,)), dma((groups,)),
-            dma((pieces,)), dma((pieces,)), dma((pieces,)),
+            dma((TILES,)), dma((TILES,)), dma((TILES,)),
+            dma((TILES + 1,)), dma((TILES + 1,)), dma((TILES + 1,)),
         ],
         compiler_params=pltpu.CompilerParams(
-            collective_id=0, has_side_effects=True, vmem_limit_bytes=40 * 1024 * 1024
+            collective_id=0, has_side_effects=True, vmem_limit_bytes=65400 * 1024
         ),
         name="wave_step",
     )(
@@ -679,7 +675,6 @@
         sea_mask,
         sea_cell.reshape(48, 128),
         slab_counts,
-        jnp.asarray(np.stack([COS, SIN])),
     ).transpose(1, 0, 2)
 
 

time: 109 us -> 92.1 us (0.84)
  Pallas kernels: 103 us -> 89.8 us
  local copies, waits for them, and re-layouts: 5.77 us -> 2.14 us
    pallas_call x1, Pallas kernels: 103 us -> 89.8 us  [per_device(): pl.pallas_call(kernel, out_shape=jax.ShapeDtypeStruct((ND, NC, SLOTS), f3...]
    unnamed x15 -> x1, local copies, waits for them, and re-layouts: 5.77 us -> 2.14 us
where the time goes in v2:
time: 92.1 us; the launch traced here: 92 us
  Pallas kernels  89.8 us (98%)
  local copies, waits for them, and re-layouts  2.14 us (2%)
    pallas_call x1, Pallas kernels, per_device(): pl.pallas_call(kernel, out_shape=jax.ShapeDtypeStruct((ND, NC, SLOTS), f3...  89.8 us
    unnamed x1, local copies, waits for them, and re-layouts  2.14 us

profile of v2, /device:TPU:1, one launch (start us, length us, event | category | flops | bytes accessed | tf_op | source)
XLA Modules:
  0.0 92.0 jit_solution(3476449486504784794)
XLA Ops:
  0.0 89.8 %wave_step.1 = f32[36,8,768]{2,1,0:T(8,128)} custom-call(f32[36,8,768]{2,1,0:T(8,128)} %bitcast.4, f32[1,8,1024]{2,1,0:T(8,128)} %speed_in.1, f32[1,8,1024]{2,1,0:T(8,128)} %turn_in.1, s32[8,1024]{1,0:T(8,128)} %mask_in.1, s32[48,128]{1,0:T(8,128)} %bitcast.5, s32[32]{0:T(128)} %counts_in.1), custom_call_target="tpu_custom_call" | custom-call | tf_op jit(solution)/shard_map/wave_step/pallas_call | solution.py:624
  89.8 2.1 %copy.8 = f32[8,36,768]{2,0,1:T(8,128)} copy(f32[8,36,768]{2,0,1:T(8,128)} %bitcast.3) | data formatting | bytes 1769472

commit v3 on v2

--- a/solution.py
+++ b/solution.py
@@ -280,13 +280,6 @@
     for k in range(4):
         stat_copy(k).start()
 
-    for k in range(4):
-        stat_copy(k).wait()
-    south_mask = jnp.where(me_l > 0, stat_halo[1], 0.0)
-    north_mask = jnp.where(me_l < NL - 1, stat_halo[3], 0.0)
-    sy[0] = 0.5 * (stat_halo[0] + spd[0:8, :]) * south_mask * msk[0:8, :]
-    sy[8] = 0.5 * (stat_halo[2] + spd[56:64, :]) * north_mask * msk[56:64, :]
-
     def a_rows(direction):
         return [a_buf[direction, :, pl.ds(128 * u, 128)] for u in range(6)]
 
@@ -343,6 +336,13 @@
         w_last[v] = windows(LAST, v, rows)
     lax.fori_loop(0, TILES, pack_tile, 0)
 
+    for k in range(4):
+        stat_copy(k).wait()
+    south_mask = jnp.where(me_l > 0, stat_halo[1], 0.0)
+    north_mask = jnp.where(me_l < NL - 1, stat_halo[3], 0.0)
+    sy[0] = 0.5 * (stat_halo[0] + spd[0:8, :]) * south_mask * msk[0:8, :]
+    sy[8] = 0.5 * (stat_halo[2] + spd[56:64, :]) * north_mask * msk[56:64, :]
+
     r_rows = r_buf.reshape(TILES, NL * 8, 128)
 
     def turn_points(tile, carry):
@@ -351,8 +351,6 @@
         for h in range(2):
             p_buf[tile, h] = r_rows[tile, pl.ds(h, 128, stride=2), :].T
         return carry
-
-    lax.fori_loop(0, TILES, turn_points, 0)
 
     def point_rows(tile, s, u, h):
         if s is None:
@@ -374,69 +372,103 @@
             q = jnp.where(msk[pl.ds(8 * v, 8), :] > 0.0, lanes(value, lane_at[v]), 0.0)
             x_ext[0, direction, v + 2] = sweep_x(q, cosine * sx[v], sign, sub, lane)
 
-    def place_tile(tile, carry):
-        for s in range(FOLD):
-            place(FOLD * tile + s, tile, s)
-        return carry
-
-    lax.fori_loop(0, TILES, place_tile, 0)
-    place(LAST, None, None)
-
-    def halo_copy(step, k):
+    def halo_copy(step, dirs, rows, to_north, k):
+        source_row = 2 + ROWS - rows if to_north else 2
+        target_row = 2 - rows if to_north else 2 + ROWS
+        return pltpu.make_async_remote_copy(
+            src_ref=x_ext.at[step, dirs, pl.ds(source_row, rows)],
+            dst_ref=x_ext.at[step, dirs, pl.ds(target_row, rows)],
+            send_sem=halo_send.at[step, k],
+            recv_sem=halo_recv.at[step, k],
+            device_id=north if to_north else south,
+            device_id_type=pl.DeviceIdType.MESH,
+        )
+
+    def tile_halos(tile, kind):
+        north_rows, south_rows = ((2, 1), (2, 2), (1, 2))[kind]
+        dirs = pl.ds(FOLD * tile, 1 if isinstance(tile, int) and tile == TILES else FOLD)
+        return (
+            halo_copy(0, dirs, north_rows, True, 2 * tile),
+            halo_copy(0, dirs, south_rows, False, 2 * tile + 1),
+        )
+
+    def second_halos():
         positive = pl.ds(0, SIN_POS)
         negative = pl.ds(SIN_POS, ND - SIN_POS)
-        which, source_rows, target_rows, peer = (
-            (positive, pl.ds(8, 2), pl.ds(0, 2), north),
-            (negative, pl.ds(9, 1), pl.ds(1, 1), north),
-            (positive, pl.ds(2, 1), pl.ds(10, 1), south),
-            (negative, pl.ds(2, 2), pl.ds(10, 2), south),
-        )[k]
-        return pltpu.make_async_remote_copy(
-            src_ref=x_ext.at[step, which, source_rows],
-            dst_ref=x_ext.at[step, which, target_rows],
-            send_sem=halo_send.at[step, k],
-            recv_sem=halo_recv.at[step, k],
-            device_id=peer,
-            device_id_type=pl.DeviceIdType.MESH,
-        )
-
-    def sweep_y(step, positive, row_list):
-        def body(direction, carry):
-            sine = trig[1, direction]
-
-            def row(r):
-                value = x_ext[step, direction, r + 2]
-                if r < 0:
-                    value = jnp.where(me_l > 0, value, 0.0)
-                if r >= ROWS:
-                    value = jnp.where(me_l < NL - 1, value, 0.0)
-                return value
-
-            diffs = {}
-            fluxes = {}
-
-            def diff(f):
-                if f not in diffs:
-                    diffs[f] = row(f) - row(f - 1)
-                return diffs[f]
-
-            def face(f):
-                if f not in fluxes:
-                    if positive:
-                        curvature = diff(f) - diff(f - 1)
-                    else:
-                        curvature = diff(f + 1) - diff(f)
-                    fluxes[f] = flux(row(f - 1), diff(f), curvature, sine * sy[f])
-                return fluxes[f]
-
-            for r in row_list:
-                y_buf[direction, r] = row(r) - (face(r + 1) - face(r))
+        return (
+            halo_copy(1, positive, 2, True, 0),
+            halo_copy(1, negative, 1, True, 1),
+            halo_copy(1, positive, 1, False, 2),
+            halo_copy(1, negative, 2, False, 3),
+        )
+
+    def sweep_y(step, direction, positive, row_list):
+        sine = trig[1, direction]
+
+        def row(r):
+            value = x_ext[step, direction, r + 2]
+            if r < 0:
+                value = jnp.where(me_l > 0, value, 0.0)
+            if r >= ROWS:
+                value = jnp.where(me_l < NL - 1, value, 0.0)
+            return value
+
+        diffs = {}
+        fluxes = {}
+
+        def diff(f):
+            if f not in diffs:
+                diffs[f] = row(f) - row(f - 1)
+            return diffs[f]
+
+        def face(f):
+            if f not in fluxes:
+                if positive:
+                    curvature = diff(f) - diff(f - 1)
+                else:
+                    curvature = diff(f + 1) - diff(f)
+                fluxes[f] = flux(row(f - 1), diff(f), curvature, sine * sy[f])
+            return fluxes[f]
+
+        for r in row_list:
+            y_buf[direction, r] = row(r) - (face(r + 1) - face(r))
+
+    def sweep_y_all(step, row_list):
+        def body(positive):
+            def one(direction, carry):
+                sweep_y(step, direction, positive, row_list)
+                return carry
+
+            return one
+
+        lax.fori_loop(0, SIN_POS, body(True), 0)
+        lax.fori_loop(SIN_POS, ND, body(False), 0)
+
+    inner = tuple(range(2, 6))
+    outer = (0, 1, 6, 7)
+
+    def receive_tile(kind):
+        def body(tile, carry):
+            turn_points(tile, 0)
+            for s in range(FOLD):
+                place(FOLD * tile + s, tile, s)
+            for copy in tile_halos(tile, kind):
+                copy.start()
+            for s in range(FOLD):
+                positive = kind == 0 or (kind == 1 and FOLD * tile + s < SIN_POS)
+                sweep_y(0, FOLD * tile + s, positive, inner)
             return carry
 
-        if positive:
-            lax.fori_loop(0, SIN_POS, body, 0)
-        else:
-            lax.fori_loop(SIN_POS, ND, body, 0)
+        return body
+
+    middle = SIN_POS // FOLD
+    lax.fori_loop(0, middle, receive_tile(0), 0)
+    place(LAST, None, None)
+    for copy in tile_halos(TILES, 2):
+        copy.start()
+    sweep_y(0, LAST, False, inner)
+    receive_tile(1)(middle, 0)
+    lax.fori_loop(middle + 1, TILES, receive_tile(2), 0)
 
     def sweep_theta(step, r):
         t = trn[pl.ds(pl.multiple_of(8 * r, 8), 8), :]
@@ -465,28 +497,34 @@
             else:
                 y_buf[j, r] = value
 
-    inner = tuple(range(2, 6))
-    outer = (0, 1, 6, 7)
-    for step in range(2):
-        for k in range(4):
-            halo_copy(step, k).start()
-        sweep_y(step, True, inner)
-        sweep_y(step, False, inner)
-
-        def inner_rows(r, carry, step=step):
+    def theta_inner(step):
+        def body(r, carry):
             sweep_theta(step, r)
             return carry
 
-        def outer_rows(k, carry, step=step):
+        lax.fori_loop(2, 6, body, 0)
+
+    def theta_outer(step):
+        def body(k, carry):
             sweep_theta(step, k + 4 * (k // 2))
             return carry
 
-        lax.fori_loop(2, 6, inner_rows, 0)
-        for k in range(4):
-            halo_copy(step, k).wait()
-        sweep_y(step, True, outer)
-        sweep_y(step, False, outer)
-        lax.fori_loop(0, 4, outer_rows, 0)
+        lax.fori_loop(0, 4, body, 0)
+
+    theta_inner(0)
+    for tile in range(TILES + 1):
+        for copy in tile_halos(tile, 0 if tile < middle else 1 if tile == middle else 2):
+            copy.wait()
+    sweep_y_all(0, outer)
+    theta_outer(0)
+    for copy in second_halos():
+        copy.start()
+    sweep_y_all(1, inner)
+    theta_inner(1)
+    for copy in second_halos():
+        copy.wait()
+    sweep_y_all(1, outer)
+    theta_outer(1)
 
     def collect(direction, tile, s):
         taken = [lanes(y_buf[direction, v], take_at[v]) for v in range(ROWS)]
@@ -623,7 +661,7 @@
     anywhere = pl.BlockSpec(memory_space=pl.ANY)
     return pl.pallas_call(
         kernel,
-        out_shape=jax.ShapeDtypeStruct((ND, NC, SLOTS), f32),
+        out_shape=pltpu.VMEM((ND, NC, SLOTS), f32),
         in_specs=[hbm] * 6,
         out_specs=anywhere,
         scratch_shapes=[
@@ -660,12 +698,12 @@
             pltpu.VMEM((TILES,) + vreg, f32),
             dma((TILES + 1,)), dma((TILES + 1,)), dma((TILES + 1,)),
             dma((TILES,)), dma((TILES,)), dma((TILES,)),
-            dma((4,)), dma((4,)), dma((2, 4)), dma((2, 4)),
+            dma((4,)), dma((4,)), dma((2, 2 * TILES + 2)), dma((2, 2 * TILES + 2)),
             dma((TILES,)), dma((TILES,)), dma((TILES,)),
             dma((TILES + 1,)), dma((TILES + 1,)), dma((TILES + 1,)),
         ],
         compiler_params=pltpu.CompilerParams(
-            collective_id=0, has_side_effects=True, vmem_limit_bytes=65400 * 1024
+            collective_id=0, has_side_effects=True, vmem_limit_bytes=64000 * 1024
         ),
         name="wave_step",
     )(

time: 92.1 us -> 83.8 us (0.910)
  Pallas kernels: 89.8 us -> 82.7 us
  local copies, waits for them, and re-layouts: 2.14 us -> 0.91 us
    pallas_call x1, Pallas kernels: 89.8 us -> 82.7 us  [per_device(): pl.pallas_call(kernel, out_shape=pltpu.VMEM((ND, NC, SLOTS), f32), in_spe...]
    unnamed x1, local copies, waits for them, and re-layouts: 2.14 us -> 0.91 us
where the time goes in v3:
time: 83.8 us; the launch traced here: 83.6 us
  Pallas kernels  82.7 us (99%)
  local copies, waits for them, and re-layouts  0.91 us (1%)
    pallas_call x1, Pallas kernels, per_device(): pl.pallas_call(kernel, out_shape=pltpu.VMEM((ND, NC, SLOTS), f32), in_spe...  82.7 us

profile of v3, /device:TPU:1, one launch (start us, length us, event | category | flops | bytes accessed | tf_op | source)
XLA Modules:
  0.0 83.6 jit_solution(16255981792744967315)
XLA Ops:
  0.0 82.7 %wave_step.1 = f32[36,8,768]{2,1,0:T(8,128)S(1)} custom-call(f32[36,8,768]{2,1,0:T(8,128)} %bitcast.4, f32[1,8,1024]{2,1,0:T(8,128)} %speed_in.1, f32[1,8,1024]{2,1,0:T(8,128)} %turn_in.1, s32[8,1024]{1,0:T(8,128)} %mask_in.1, s32[48,128]{1,0:T(8,128)} %bitcast.5, s32[32]{0:T(128)} %counts_in.1), custom_call_target="tpu_custom_call" | custom-call | tf_op jit(solution)/shard_map/wave_step/pallas_call | solution.py:662
  82.7 0.9 %copy.8 = f32[8,36,768]{2,0,1:T(8,128)} copy(f32[8,36,768]{2,0,1:T(8,128)S(1)} %bitcast.3) | data formatting | bytes 1769472

commit v4 on v3

--- a/solution.py
+++ b/solution.py
@@ -16,6 +16,7 @@
 ROWS = 8
 FOLD = 5
 TILES = 7
+EARLY = 3
 LAST = ND - 1
 SIN_POS = 19
 
@@ -87,10 +88,11 @@
 def kernel(
     spectra, speed_in, turn_in, mask_in, cells_in, counts_in, out,
     speed, turn, mask, cells, counts, trig, load_sem,
-    a_buf, m_buf, r_buf, p_buf, n_buf, o_buf, x_ext, y_buf,
+    a_buf, own_buf, m_buf, x_buf, r_buf, p_buf, z_buf, n_buf, o_buf, x_ext, y_buf,
     spd, trn, msk, stat_halo, sx, sy,
-    pack_at, put_at, put_tile, row_at, row_tile, lane_at, take_at, back_row, back_tile, w_last,
+    pack_at, own_at, put_at, put_tile, own_put_at, own_put_tile, row_at, row_tile, lane_at, take_at, back_row, back_tile, w_last,
     first_send, first_recv, first_own, second_send, second_recv, second_own,
+    cross_send, cross_recv, cross_own, back_send, back_recv, back_own,
     stat_send, stat_recv, halo_send, halo_recv,
     third_send, third_recv, third_own, fourth_send, fourth_recv, fourth_own,
 ):
@@ -104,14 +106,22 @@
     loads = [
         pltpu.make_async_copy(source_ref, target_ref, load_sem.at[k])
         for k, (source_ref, target_ref) in enumerate(
-            ((counts_in, counts), (speed_in, speed), (turn_in, turn), (mask_in, mask), (cells_in, cells))
+            (
+                (counts_in, counts),
+                (spectra.at[pl.ds(0, FOLD * EARLY)], own_buf.at[pl.ds(0, FOLD * EARLY)]),
+                (spectra.at[pl.ds(LAST, 1)], own_buf.at[pl.ds(LAST, 1)]),
+                (speed_in, speed),
+                (turn_in, turn),
+                (mask_in, mask),
+                (cells_in, cells),
+            )
         )
     ]
     for load in loads:
         load.start()
 
-    def chunk(g):
-        return pl.ds(FOLD * g, 1 if isinstance(g, int) and g == TILES else FOLD)
+    def chunk(tile):
+        return pl.ds(FOLD * tile, FOLD)
 
     def first_ends(g, peer):
         return spectra.at[chunk(g), peer, :], a_buf.at[chunk(g), slot_of(me_c), :]
@@ -120,7 +130,7 @@
         source_ref, target_ref = first_ends(g, me_c)
         return pltpu.make_async_copy(source_ref, target_ref, first_own.at[g])
 
-    for g in range(TILES + 1):
+    for g in range(EARLY, TILES):
         first_local(g).start()
 
     barrier = pltpu.get_barrier_semaphore()
@@ -154,6 +164,7 @@
         own_start = own_start + jnp.where(slab < me_l, counts[slab], 0)
 
     source = ((sub & 1) * 4 + (sub >> 1)) * NL + me_l
+    own_source = me_c * NL + me_l
     block = (lane * 171) >> 12
     in_block = lane - block * BUCKET
     block_masks = [block == b for b in range(FOLD)]
@@ -167,6 +178,7 @@
             if FOLD * v + b < NL:
                 base = jnp.where(block == b, starts[FOLD * v + b], base)
         pack_at[v] = ((base - source + 255) >> 8) + in_block
+        own_at[v] = ((base - own_source + 255) >> 8) + in_block
 
     for t in range(8):
         columns = pl.ds(128 * t, 128)
@@ -175,17 +187,18 @@
         msk[pl.ds(t, 8, stride=8), :] = mask[:, columns].astype(jnp.float32)
 
     for u in range(6):
-        point = source + (lane + 128 * u) * 256
-        slab = jnp.zeros((8, 128), jnp.int32)
-        begin = jnp.zeros((8, 128), jnp.int32)
-        for s in range(1, NL + 1):
-            past = point >= starts[s]
-            slab = jnp.where(past, s, slab)
-            begin = jnp.where(past, starts[s], begin)
-        nth = lane + 128 * u - ((begin - source + 255) >> 8)
-        tile = (slab * 205) >> 10
-        put_at[u] = ((slab - tile * FOLD) * BUCKET + nth) & 127
-        put_tile[u] = jnp.where(slab < NL, tile, -1)
+        for origin, at, which in ((source, put_at, put_tile), (own_source, own_put_at, own_put_tile)):
+            point = origin + (lane + 128 * u) * 256
+            slab = jnp.zeros((8, 128), jnp.int32)
+            begin = jnp.zeros((8, 128), jnp.int32)
+            for s in range(1, NL + 1):
+                past = point >= starts[s]
+                slab = jnp.where(past, s, slab)
+                begin = jnp.where(past, starts[s], begin)
+            nth = lane + 128 * u - ((begin - origin + 255) >> 8)
+            tile = (slab * 205) >> 10
+            at[u] = ((slab - tile * FOLD) * BUCKET + nth) & 127
+            which[u] = jnp.where(slab < NL, tile, -1)
 
     ones = jnp.ones((128, 128), jnp.bfloat16)
     deep = lax.broadcasted_iota(jnp.int32, (128, 128), 0)
@@ -258,7 +271,7 @@
             device_id_type=pl.DeviceIdType.MESH,
         )
 
-    for g in (TILES,) + tuple(range(TILES)):
+    for g in range(EARLY, TILES):
         for r in range(1, NC):
             first_copy(g, r).start()
 
@@ -280,11 +293,11 @@
     for k in range(4):
         stat_copy(k).start()
 
-    def a_rows(direction):
-        return [a_buf[direction, :, pl.ds(128 * u, 128)] for u in range(6)]
-
-    def windows(direction, v, rows):
-        at = pack_at[v]
+    def slot_rows(buffer, direction):
+        return [buffer[direction, :, pl.ds(128 * u, 128)] for u in range(6)]
+
+    def windows(at_ref, v, rows):
+        at = at_ref[v]
         low = at & 127
         value = None
         for u in SLOT_TILES[v]:
@@ -292,49 +305,90 @@
             value = got if value is None else jnp.where((at >> 7) == u, got, value)
         return value
 
-    def second_copy(tile, r):
+    def second_copy(tile, r, early):
         peer = (me_l + r) % NL
         return pltpu.make_async_remote_copy(
             src_ref=m_buf.at[peer, tile],
-            dst_ref=r_buf.at[tile, me_l],
+            dst_ref=x_buf.at[tile, me_l] if early else r_buf.at[tile, me_l],
             send_sem=second_send.at[tile],
             recv_sem=second_recv.at[tile],
             device_id={"comp": me_c, "lat": peer},
             device_id_type=pl.DeviceIdType.MESH,
         )
 
-    def second_local(tile):
-        return pltpu.make_async_copy(m_buf.at[me_l, tile], r_buf.at[tile, me_l], second_own.at[tile])
+    def second_local(tile, early):
+        return pltpu.make_async_copy(
+            m_buf.at[me_l, tile],
+            x_buf.at[tile, me_l] if early else r_buf.at[tile, me_l],
+            second_own.at[tile],
+        )
 
     def many(ref, tile, sem):
         part = ref.at[tile, pl.ds(0, NL - 1)]
         return pltpu.make_async_copy(part, part, sem.at[tile])
 
-    def pack_tile(tile, carry):
-        arrived(tile)
-        rows = [a_rows(FOLD * tile + s) for s in range(FOLD)]
-        octet = jnp.minimum(tile, 2) * 8
-        for v in range(TILES):
-            parts = [windows(FOLD * tile + s, v, rows[s]) for s in range(FOLD)]
-            spare = w_last[v]
-            for b, value in enumerate(swap_blocks(parts, block_masks, turns)):
-                if FOLD * v + b < NL:
-                    extra = lanes(spare, BUCKET * b + octet + (lane & 7))
-                    m_buf[FOLD * v + b, tile] = jnp.where(lane >= 120, extra, value)
-        for r in range(1, NL):
-            second_copy(tile, r).start()
-        second_local(tile).start()
+    def pack_tile(early):
+        def body(tile, carry):
+            if early:
+                buffer, at_ref = own_buf, own_at
+            else:
+                buffer, at_ref = a_buf, pack_at
+                first_wait(tile, first_recv).wait()
+                first_local(tile).wait()
+            rows = [slot_rows(buffer, FOLD * tile + s) for s in range(FOLD)]
+            for v in range(TILES):
+                parts = [windows(at_ref, v, rows[s]) for s in range(FOLD)]
+                for b, value in enumerate(swap_blocks(parts, block_masks, turns)):
+                    if FOLD * v + b < NL:
+                        if early:
+                            extra = lanes(w_last[v], BUCKET * b + 8 * tile + (lane & 7))
+                            value = jnp.where(lane >= 120, extra, value)
+                        m_buf[FOLD * v + b, tile] = value
+            for r in range(1, NL):
+                second_copy(tile, r, early).start()
+            second_local(tile, early).start()
+            return carry
+
+        return body
+
+    last_rows = slot_rows(own_buf, LAST)
+    for v in range(TILES):
+        w_last[v] = windows(own_at, v, last_rows)
+    lax.fori_loop(0, EARLY, pack_tile(True), 0)
+    lax.fori_loop(EARLY, TILES, pack_tile(False), 0)
+
+    def cross_ends(tile, peer):
+        return x_buf.at[tile, :, peer, :], r_buf.at[tile, :, slot_of(me_c), :]
+
+    def cross_copy(tile, r):
+        peer = (me_c + r) % NC
+        source_ref, target_ref = cross_ends(tile, peer)
+        return pltpu.make_async_remote_copy(
+            src_ref=source_ref,
+            dst_ref=target_ref,
+            send_sem=cross_send.at[tile],
+            recv_sem=cross_recv.at[tile],
+            device_id={"comp": peer, "lat": me_l},
+            device_id_type=pl.DeviceIdType.MESH,
+        )
+
+    def cross_local(tile):
+        source_ref, target_ref = cross_ends(tile, me_c)
+        return pltpu.make_async_copy(source_ref, target_ref, cross_own.at[tile])
+
+    def cross_many(ref, tile, sem):
+        part = ref.at[tile, :, pl.ds(0, NC - 1), :]
+        return pltpu.make_async_copy(part, part, sem.at[tile])
+
+    def cross_tile(tile, carry):
+        many(x_buf, tile, second_recv).wait()
+        second_local(tile, True).wait()
+        for r in range(1, NC):
+            cross_copy(tile, r).start()
+        cross_local(tile).start()
         return carry
 
-    def arrived(g):
-        first_wait(g, first_recv).wait()
-        first_local(g).wait()
-
-    arrived(TILES)
-    rows = a_rows(LAST)
-    for v in range(TILES):
-        w_last[v] = windows(LAST, v, rows)
-    lax.fori_loop(0, TILES, pack_tile, 0)
+    lax.fori_loop(0, EARLY, cross_tile, 0)
 
     for k in range(4):
         stat_copy(k).wait()
@@ -345,12 +399,15 @@
 
     r_rows = r_buf.reshape(TILES, NL * 8, 128)
 
-    def turn_points(tile, carry):
-        many(r_buf, tile, second_recv).wait()
-        second_local(tile).wait()
+    def turn_points(tile, early):
+        if early:
+            cross_many(r_buf, tile, cross_recv).wait()
+            cross_local(tile).wait()
+        else:
+            many(r_buf, tile, second_recv).wait()
+            second_local(tile, False).wait()
         for h in range(2):
             p_buf[tile, h] = r_rows[tile, pl.ds(h, 128, stride=2), :].T
-        return carry
 
     def point_rows(tile, s, u, h):
         if s is None:
@@ -449,7 +506,7 @@
 
     def receive_tile(kind):
         def body(tile, carry):
-            turn_points(tile, 0)
+            turn_points(tile, kind == 0)
             for s in range(FOLD):
                 place(FOLD * tile + s, tile, s)
             for copy in tile_halos(tile, kind):
@@ -462,6 +519,7 @@
         return body
 
     middle = SIN_POS // FOLD
+    assert middle == EARLY
     lax.fori_loop(0, middle, receive_tile(0), 0)
     place(LAST, None, None)
     for copy in tile_halos(TILES, 2):
@@ -541,51 +599,91 @@
                 else:
                     p_buf[tile, h, BUCKET * s + 8 * u : BUCKET * s + 8 * u + 8, :] = value
 
-    def third_copy(tile, r):
+    def third_ends(tile, peer, early):
+        source_ref = z_buf.at[tile, peer] if early else r_buf.at[tile, peer]
+        return source_ref, n_buf.at[tile, me_l]
+
+    def third_copy(tile, r, early):
         peer = (me_l + r) % NL
+        source_ref, target_ref = third_ends(tile, peer, early)
         return pltpu.make_async_remote_copy(
-            src_ref=m_buf.at[peer, tile],
-            dst_ref=n_buf.at[tile, me_l],
+            src_ref=source_ref,
+            dst_ref=target_ref,
             send_sem=third_send.at[tile],
             recv_sem=third_recv.at[tile],
             device_id={"comp": me_c, "lat": peer},
             device_id_type=pl.DeviceIdType.MESH,
         )
 
-    def third_local(tile):
-        return pltpu.make_async_copy(m_buf.at[me_l, tile], n_buf.at[tile, me_l], third_own.at[tile])
-
-    for tile in range(TILES):
-        many(r_buf, tile, second_send).wait()
-
-    def turn_out(tile, carry):
-        for h in range(2):
-            r_rows[tile, pl.ds(h, 128, stride=2), :] = p_buf[tile, h].T
-        for l in range(NL):
-            m_buf[l, tile] = r_buf[tile, l]
+    def third_local(tile, early):
+        source_ref, target_ref = third_ends(tile, me_l, early)
+        return pltpu.make_async_copy(source_ref, target_ref, third_own.at[tile])
+
+    def third_send_all(tile, early):
+        for r in range(1, NL):
+            third_copy(tile, r, early).start()
+        third_local(tile, early).start()
+
+    def back_ends(tile, peer):
+        return r_buf.at[tile, :, slot_of(peer), :], z_buf.at[tile, :, me_c, :]
+
+    def back_copy(tile, r):
+        peer = (me_c + r) % NC
+        source_ref, target_ref = back_ends(tile, peer)
+        return pltpu.make_async_remote_copy(
+            src_ref=source_ref,
+            dst_ref=target_ref,
+            send_sem=back_send.at[tile],
+            recv_sem=back_recv.at[tile],
+            device_id={"comp": peer, "lat": me_l},
+            device_id_type=pl.DeviceIdType.MESH,
+        )
+
+    def back_local(tile):
+        source_ref, target_ref = back_ends(tile, me_c)
+        return pltpu.make_async_copy(source_ref, target_ref, back_own.at[tile])
+
+    def collect_tile(early):
+        def body(tile, carry):
+            for s in range(FOLD):
+                collect(FOLD * tile + s, tile, s)
+            for h in range(2):
+                r_rows[tile, pl.ds(h, 128, stride=2), :] = p_buf[tile, h].T
+            if early:
+                for r in range(1, NC):
+                    back_copy(tile, r).start()
+                back_local(tile).start()
+            else:
+                third_send_all(tile, False)
+            return carry
+
+        return body
+
+    def back_tile_on(tile, carry):
+        cross_many(z_buf, tile, back_recv).wait()
+        back_local(tile).wait()
+        third_send_all(tile, True)
         return carry
 
-    def collect_tile(tile, carry):
-        for s in range(FOLD):
-            collect(FOLD * tile + s, tile, s)
-        turn_out(tile, 0)
-        for r in range(1, NL):
-            third_copy(tile, r).start()
-        third_local(tile).start()
-        return carry
-
+    lax.fori_loop(EARLY, EARLY + 1, collect_tile(False), 0)
     collect(LAST, None, None)
-    lax.fori_loop(0, TILES, collect_tile, 0)
-
-    def put(direction, parts):
+    lax.fori_loop(0, EARLY, collect_tile(True), 0)
+    lax.fori_loop(EARLY + 1, TILES, collect_tile(False), 0)
+    lax.fori_loop(0, EARLY, back_tile_on, 0)
+
+    def put(direction, parts, early):
         for u in range(6):
-            at = put_at[u]
-            which = put_tile[u]
+            at = own_put_at[u] if early else put_at[u]
+            which = own_put_tile[u] if early else put_tile[u]
             value = jnp.zeros((8, 128), jnp.float32)
             for v in range(TILES):
                 if u in SLOT_TILES[v]:
                     value = jnp.where(which == v, lanes(parts[v], at), value)
-            o_buf[direction, :, pl.ds(128 * u, 128)] = value
+            columns = pl.ds(128 * u, 128)
+            if early:
+                out[direction, :, columns] = value
+            else:
+                o_buf[direction, :, columns] = value
 
     def fourth_ends(k, peer):
         part = chunk(k)
@@ -612,17 +710,21 @@
             fourth_copy(k, r).start()
         fourth_local(k).start()
 
-    def put_tile_of(tile, carry):
-        many(n_buf, tile, third_recv).wait()
-        third_local(tile).wait()
-        swapped = []
-        for v in range(TILES):
-            parts = [n_buf[tile, min(FOLD * v + b, NL - 1)] for b in range(FOLD)]
-            swapped.append(swap_blocks(parts, block_masks, turns))
-        for s in range(FOLD):
-            put(FOLD * tile + s, [swapped[v][s] for v in range(TILES)])
-        fourth_send_all(tile)
-        return carry
+    def put_tile_of(early):
+        def body(tile, carry):
+            many(n_buf, tile, third_recv).wait()
+            third_local(tile, early).wait()
+            swapped = []
+            for v in range(TILES):
+                parts = [n_buf[tile, min(FOLD * v + b, NL - 1)] for b in range(FOLD)]
+                swapped.append(swap_blocks(parts, block_masks, turns))
+            for s in range(FOLD):
+                put(FOLD * tile + s, [swapped[v][s] for v in range(TILES)], early)
+            if not early:
+                fourth_send_all(tile)
+            return carry
+
+        return body
 
     def put_last():
         parts = []
@@ -635,18 +737,21 @@
                         got = lanes(n_buf[e, FOLD * v + b], spare)
                         value = jnp.where((lane >> 3) == 3 * b + e, got, value)
             parts.append(value)
-        put(LAST, parts)
-
-    lax.fori_loop(0, 3, put_tile_of, 0)
+        put(LAST, parts, True)
+
+    lax.fori_loop(EARLY, TILES, put_tile_of(False), 0)
+    lax.fori_loop(0, EARLY, put_tile_of(True), 0)
     put_last()
-    fourth_send_all(TILES)
-    lax.fori_loop(3, TILES, put_tile_of, 0)
-
-    for g in range(TILES + 1):
+
+    for g in range(EARLY, TILES):
         first_wait(g, first_send).wait()
     for tile in range(TILES):
+        many(r_buf, tile, second_send).wait()
         many(n_buf, tile, third_send).wait()
-    for k in range(TILES + 1):
+    for tile in range(EARLY):
+        cross_many(r_buf, tile, cross_send).wait()
+        cross_many(z_buf, tile, back_send).wait()
+    for k in range(EARLY, TILES):
         fourth_local(k).wait()
         part = out.at[chunk(k), pl.ds(0, NC - 1), :]
         pltpu.make_async_copy(part, part, fourth_recv.at[k]).wait()
@@ -658,12 +763,11 @@
     vreg = (8, 128)
     dma = pltpu.SemaphoreType.DMA
     hbm = pl.BlockSpec(memory_space=pltpu.HBM)
-    anywhere = pl.BlockSpec(memory_space=pl.ANY)
     return pl.pallas_call(
         kernel,
         out_shape=pltpu.VMEM((ND, NC, SLOTS), f32),
         in_specs=[hbm] * 6,
-        out_specs=anywhere,
+        out_specs=pl.BlockSpec(memory_space=pltpu.VMEM),
         scratch_shapes=[
             pltpu.VMEM((1, ROWS, 1024), f32),
             pltpu.VMEM((1, ROWS, 1024), f32),
@@ -671,11 +775,14 @@
             pltpu.VMEM((48, 128), jnp.int32),
             pltpu.SMEM((NL,), jnp.int32),
             pltpu.SMEM((2, ND), f32),
-            dma((5,)),
+            dma((7,)),
+            pltpu.VMEM((ND, NC, SLOTS), f32),
             pltpu.VMEM((ND, NC, SLOTS), f32),
             pltpu.VMEM((NL, TILES) + vreg, f32),
+            pltpu.VMEM((EARLY, NL) + vreg, f32),
             pltpu.VMEM((TILES, NL) + vreg, f32),
             pltpu.VMEM((TILES, 2, 128, 128), f32),
+            pltpu.VMEM((EARLY, NL) + vreg, f32),
             pltpu.VMEM((TILES, NL) + vreg, f32),
             pltpu.VMEM((ND, NC, SLOTS), f32),
             pltpu.VMEM((2, ND, ROWS + 4) + vreg, f32),
@@ -687,6 +794,9 @@
             pltpu.VMEM((ROWS,) + vreg, f32),
             pltpu.VMEM((ROWS + 1,) + vreg, f32),
             pltpu.VMEM((TILES,) + vreg, jnp.int32),
+            pltpu.VMEM((TILES,) + vreg, jnp.int32),
+            pltpu.VMEM((6,) + vreg, jnp.int32),
+            pltpu.VMEM((6,) + vreg, jnp.int32),
             pltpu.VMEM((6,) + vreg, jnp.int32),
             pltpu.VMEM((6,) + vreg, jnp.int32),
             pltpu.VMEM((ROWS,) + vreg, jnp.int32),
@@ -696,11 +806,13 @@
             pltpu.VMEM((3, 2) + vreg, jnp.int32),
             pltpu.VMEM((3, 2) + vreg, jnp.int32),
             pltpu.VMEM((TILES,) + vreg, f32),
-            dma((TILES + 1,)), dma((TILES + 1,)), dma((TILES + 1,)),
             dma((TILES,)), dma((TILES,)), dma((TILES,)),
+            dma((TILES,)), dma((TILES,)), dma((TILES,)),
+            dma((EARLY,)), dma((EARLY,)), dma((EARLY,)),
+            dma((EARLY,)), dma((EARLY,)), dma((EARLY,)),
             dma((4,)), dma((4,)), dma((2, 2 * TILES + 2)), dma((2, 2 * TILES + 2)),
             dma((TILES,)), dma((TILES,)), dma((TILES,)),
-            dma((TILES + 1,)), dma((TILES + 1,)), dma((TILES + 1,)),
+            dma((TILES,)), dma((TILES,)), dma((TILES,)),
         ],
         compiler_params=pltpu.CompilerParams(
             collective_id=0, has_side_effects=True, vmem_limit_bytes=64000 * 1024

time: 83.8 us -> 71.9 us (0.86)
  Pallas kernels: 82.7 us -> 70.7 us
    pallas_call x1, Pallas kernels: 82.7 us -> 70.7 us  [per_device(): pl.pallas_call(kernel, out_shape=pltpu.VMEM((ND, NC, SLOTS), f32), in_spe...]
where the time goes in v4:
time: 71.9 us; the launch traced here: 71.6 us
  Pallas kernels  70.7 us (98%)
  local copies, waits for them, and re-layouts  0.91 us (1%)
    pallas_call x1, Pallas kernels, per_device(): pl.pallas_call(kernel, out_shape=pltpu.VMEM((ND, NC, SLOTS), f32), in_spe...  70.7 us

profile of v4, /device:TPU:1, one launch (start us, length us, event | category | flops | bytes accessed | tf_op | source)
XLA Modules:
  0.0 71.6 jit_solution(9624499619171130379)
XLA Ops:
  0.0 70.7 %wave_step.1 = f32[36,8,768]{2,1,0:T(8,128)S(1)} custom-call(f32[36,8,768]{2,1,0:T(8,128)} %bitcast.4, f32[1,8,1024]{2,1,0:T(8,128)} %speed_in.1, f32[1,8,1024]{2,1,0:T(8,128)} %turn_in.1, s32[8,1024]{1,0:T(8,128)} %mask_in.1, s32[48,128]{1,0:T(8,128)} %bitcast.5, s32[32]{0:T(128)} %counts_in.1), custom_call_target="tpu_custom_call" | custom-call | tf_op jit(solution)/shard_map/wave_step/pallas_call | solution.py:766
  70.7 0.9 %copy.8 = f32[8,36,768]{2,0,1:T(8,128)} copy(f32[8,36,768]{2,0,1:T(8,128)S(1)} %bitcast.3) | data formatting | bytes 1769472

commit v5 on v4

--- a/solution.py
+++ b/solution.py
@@ -18,6 +18,8 @@
 TILES = 7
 EARLY = 3
 LAST = ND - 1
+PARTS = ((0, 12), (12, 12), (24, 12))
+BEFORE = ((34, 16), (14, 12), (26, 8))
 SIN_POS = 19
 
 ANGLES = np.arange(ND, dtype=np.float32) * np.float32(2.0 * math.pi / ND)
@@ -31,6 +33,22 @@
     tuple(range(max(0, 4 * v - 20) // 8, min(2, (4 * v + 3) // 8) + 1)) for v in range(ROWS)
 )
 ROW_TILES = tuple(tuple(range(2 * u, min(7, 2 * u + 6) + 1)) for u in range(3))
+
+
+def ranges(first, number):
+    cuts = []
+    for j in range(first, first + number):
+        j = j % ND
+        if cuts and j == cuts[-1][0] + cuts[-1][1] and j not in (0, SIN_POS):
+            cuts[-1][1] += 1
+        else:
+            cuts.append([j, 1])
+    return [(low, size, low < SIN_POS) for low, size in cuts]
+
+
+SECOND_HALOS = [ranges(*p) for p in PARTS]
+HALOS = 2 * (TILES + 1)
+assert sum(len(r) for r in SECOND_HALOS) <= TILES + 1
 
 
 def lanes(values, index):
@@ -88,7 +106,7 @@
 def kernel(
     spectra, speed_in, turn_in, mask_in, cells_in, counts_in, out,
     speed, turn, mask, cells, counts, trig, load_sem,
-    a_buf, own_buf, m_buf, x_buf, r_buf, p_buf, z_buf, n_buf, o_buf, x_ext, y_buf,
+    a_buf, own_buf, m_buf, x_buf, r_buf, p_buf, z_buf, n_buf, o_buf, x_ext, y_buf, done,
     spd, trn, msk, stat_halo, sx, sy,
     pack_at, own_at, put_at, put_tile, own_put_at, own_put_tile, row_at, row_tile, lane_at, take_at, back_row, back_tile, w_last,
     first_send, first_recv, first_own, second_send, second_recv, second_own,
@@ -253,6 +271,39 @@
         if v < ROWS - 1:
             after = pl.ds(8 * v + 8, 8)
             sy[v + 1] = 0.5 * (s + spd[after, :]) * m * msk[after, :]
+    def slot_rows(buffer, direction):
+        return [buffer[direction, :, pl.ds(128 * u, 128)] for u in range(6)]
+
+    def windows(at_ref, v, rows):
+        at = at_ref[v]
+        low = at & 127
+        value = None
+        for u in SLOT_TILES[v]:
+            got = lanes(rows[u], low)
+            value = got if value is None else jnp.where((at >> 7) == u, got, value)
+        return value
+
+    def pack(tile, early):
+        buffer, at_ref = (own_buf, own_at) if early else (a_buf, pack_at)
+        rows = [slot_rows(buffer, FOLD * tile + s) for s in range(FOLD)]
+        for v in range(TILES):
+            parts = [windows(at_ref, v, rows[s]) for s in range(FOLD)]
+            for b, value in enumerate(swap_blocks(parts, block_masks, turns)):
+                if FOLD * v + b < NL:
+                    if early:
+                        extra = lanes(w_last[v], BUCKET * b + 8 * tile + (lane & 7))
+                        value = jnp.where(lane >= 120, extra, value)
+                    m_buf[FOLD * v + b, tile] = value
+
+    def pack_early(tile, carry):
+        pack(tile, True)
+        return carry
+
+    last_rows = slot_rows(own_buf, LAST)
+    for v in range(TILES):
+        w_last[v] = windows(own_at, v, last_rows)
+    lax.fori_loop(0, EARLY, pack_early, 0)
+
     pl.semaphore_wait(barrier, NC - 1 + NL - 1)
 
     def first_wait(g, sem):
@@ -271,9 +322,6 @@
             device_id_type=pl.DeviceIdType.MESH,
         )
 
-    for g in range(EARLY, TILES):
-        for r in range(1, NC):
-            first_copy(g, r).start()
 
     north = {"comp": me_c, "lat": (me_l + 1) % NL}
     south = {"comp": me_c, "lat": (me_l + NL - 1) % NL}
@@ -290,20 +338,6 @@
             device_id_type=pl.DeviceIdType.MESH,
         )
 
-    for k in range(4):
-        stat_copy(k).start()
-
-    def slot_rows(buffer, direction):
-        return [buffer[direction, :, pl.ds(128 * u, 128)] for u in range(6)]
-
-    def windows(at_ref, v, rows):
-        at = at_ref[v]
-        low = at & 127
-        value = None
-        for u in SLOT_TILES[v]:
-            got = lanes(rows[u], low)
-            value = got if value is None else jnp.where((at >> 7) == u, got, value)
-        return value
 
     def second_copy(tile, r, early):
         peer = (me_l + r) % NL
@@ -327,23 +361,12 @@
         part = ref.at[tile, pl.ds(0, NL - 1)]
         return pltpu.make_async_copy(part, part, sem.at[tile])
 
-    def pack_tile(early):
+    def send_tile(early):
         def body(tile, carry):
-            if early:
-                buffer, at_ref = own_buf, own_at
-            else:
-                buffer, at_ref = a_buf, pack_at
+            if not early:
                 first_wait(tile, first_recv).wait()
                 first_local(tile).wait()
-            rows = [slot_rows(buffer, FOLD * tile + s) for s in range(FOLD)]
-            for v in range(TILES):
-                parts = [windows(at_ref, v, rows[s]) for s in range(FOLD)]
-                for b, value in enumerate(swap_blocks(parts, block_masks, turns)):
-                    if FOLD * v + b < NL:
-                        if early:
-                            extra = lanes(w_last[v], BUCKET * b + 8 * tile + (lane & 7))
-                            value = jnp.where(lane >= 120, extra, value)
-                        m_buf[FOLD * v + b, tile] = value
+                pack(tile, False)
             for r in range(1, NL):
                 second_copy(tile, r, early).start()
             second_local(tile, early).start()
@@ -351,11 +374,13 @@
 
         return body
 
-    last_rows = slot_rows(own_buf, LAST)
-    for v in range(TILES):
-        w_last[v] = windows(own_at, v, last_rows)
-    lax.fori_loop(0, EARLY, pack_tile(True), 0)
-    lax.fori_loop(EARLY, TILES, pack_tile(False), 0)
+    for g in range(EARLY, TILES):
+        for r in range(1, NC):
+            first_copy(g, r).start()
+    for k in range(4):
+        stat_copy(k).start()
+    lax.fori_loop(0, EARLY, send_tile(True), 0)
+    lax.fori_loop(EARLY, TILES, send_tile(False), 0)
 
     def cross_ends(tile, peer):
         return x_buf.at[tile, :, peer, :], r_buf.at[tile, :, slot_of(me_c), :]
@@ -409,13 +434,13 @@
         for h in range(2):
             p_buf[tile, h] = r_rows[tile, pl.ds(h, 128, stride=2), :].T
 
-    def point_rows(tile, s, u, h):
+    def point_ref(tile, s, u, h):
         if s is None:
-            return p_buf[u, h, 120:128, :]
-        return p_buf[tile, h, BUCKET * s + 8 * u : BUCKET * s + 8 * u + 8, :]
+            return p_buf.at[tile[u], h, pl.ds(120, 8), :]
+        return p_buf.at[tile, h, pl.ds(pl.multiple_of(BUCKET * s + 8 * u, 8), 8), :]
 
     def place(direction, tile, s):
-        held = {(u, h): point_rows(tile, s, u, h) for u in range(3) for h in range(2)}
+        held = {(u, h): point_ref(tile, s, u, h)[...] for u in range(3) for h in range(2)}
         cosine = trig[0, direction]
         sign = jnp.where(cosine >= 0.0, 1, -1)
         for v in range(ROWS):
@@ -449,15 +474,15 @@
             halo_copy(0, dirs, south_rows, False, 2 * tile + 1),
         )
 
-    def second_halos():
-        positive = pl.ds(0, SIN_POS)
-        negative = pl.ds(SIN_POS, ND - SIN_POS)
-        return (
-            halo_copy(1, positive, 2, True, 0),
-            halo_copy(1, negative, 1, True, 1),
-            halo_copy(1, positive, 1, False, 2),
-            halo_copy(1, negative, 2, False, 3),
-        )
+    def second_halos(part):
+        k = 2 * sum(len(r) for r in SECOND_HALOS[:part])
+        copies = []
+        for low, size, positive in SECOND_HALOS[part]:
+            dirs = pl.ds(low, size)
+            copies.append(halo_copy(1, dirs, 2 if positive else 1, True, k))
+            copies.append(halo_copy(1, dirs, 1 if positive else 2, False, k + 1))
+            k += 2
+        return copies
 
     def sweep_y(step, direction, positive, row_list):
         sine = trig[1, direction]
@@ -490,19 +515,60 @@
         for r in row_list:
             y_buf[direction, r] = row(r) - (face(r + 1) - face(r))
 
-    def sweep_y_all(step, row_list):
-        def body(positive):
-            def one(direction, carry):
+    def sweep_y_of(step, cuts, row_list):
+        for low, size, positive in cuts:
+
+            def body(direction, carry, positive=positive):
                 sweep_y(step, direction, positive, row_list)
                 return carry
 
-            return one
-
-        lax.fori_loop(0, SIN_POS, body(True), 0)
-        lax.fori_loop(SIN_POS, ND, body(False), 0)
+            lax.fori_loop(low, low + size, body, 0)
+
+    def sweep_theta(step, first, number, r):
+        t = trn[pl.ds(pl.multiple_of(8 * r, 8), 8), :]
+        forward = t >= 0.0
+        q = {k: y_buf[k % ND, r] for k in range(first - 2, first + number + 2)}
+        d = {k: q[k + 1] - q[k] for k in range(first - 2, first + number + 1)}
+
+        def face(k):
+            ahead = d[k + 1] - d[k]
+            behind = d[k] - d[k - 1]
+            turning = float(TURN[k % ND])
+            if turning >= 0:
+                curvature = jnp.where(forward, behind, ahead)
+            else:
+                curvature = jnp.where(forward, ahead, behind)
+            return flux(q[k], d[k], curvature, turning * t)
+
+        prior = face(first - 1)
+        for k in range(first, first + number):
+            f = face(k)
+            value = q[k] - (f - prior)
+            prior = f
+            j = k % ND
+            if step == 0:
+                sign = 1 if COS[j] >= 0 else -1
+                x_ext[1, j, r + 2] = sweep_x(value, float(COS[j]) * sx[r], sign, sub, lane)
+            else:
+                done[j, r] = value
 
     inner = tuple(range(2, 6))
     outer = (0, 1, 6, 7)
+
+    def theta_inner(step):
+        def body(r, carry):
+            sweep_theta(step, 0, ND, r)
+            return carry
+
+        lax.fori_loop(2, 6, body, 0)
+
+    def theta_outer(step, first, number):
+        def body(k, carry):
+            sweep_theta(step, first, number, k)
+            sweep_theta(step, first, number, k + 6)
+            return carry
+
+        lax.fori_loop(0, 2, body, 0)
 
     def receive_tile(kind):
         def body(tile, carry):
@@ -521,71 +587,27 @@
     middle = SIN_POS // FOLD
     assert middle == EARLY
     lax.fori_loop(0, middle, receive_tile(0), 0)
-    place(LAST, None, None)
+    place(LAST, range(EARLY), None)
     for copy in tile_halos(TILES, 2):
         copy.start()
     sweep_y(0, LAST, False, inner)
     receive_tile(1)(middle, 0)
     lax.fori_loop(middle + 1, TILES, receive_tile(2), 0)
 
-    def sweep_theta(step, r):
-        t = trn[pl.ds(pl.multiple_of(8 * r, 8), 8), :]
-        forward = t >= 0.0
-        q = [y_buf[j, r] for j in range(ND)]
-        d = [q[(j + 1) % ND] - q[j] for j in range(ND)]
-
-        def face(j):
-            ahead = d[(j + 1) % ND] - d[j]
-            behind = d[j] - d[j - 1]
-            if TURN[j] >= 0:
-                curvature = jnp.where(forward, behind, ahead)
-            else:
-                curvature = jnp.where(forward, ahead, behind)
-            return flux(q[j], d[j], curvature, float(TURN[j]) * t)
-
-        last = face(ND - 1)
-        prior = last
-        for j in range(ND):
-            f = last if j == ND - 1 else face(j)
-            value = q[j] - (f - prior)
-            prior = f
-            if step == 0:
-                sign = 1 if COS[j] >= 0 else -1
-                x_ext[1, j, r + 2] = sweep_x(value, float(COS[j]) * sx[r], sign, sub, lane)
-            else:
-                y_buf[j, r] = value
-
-    def theta_inner(step):
-        def body(r, carry):
-            sweep_theta(step, r)
-            return carry
-
-        lax.fori_loop(2, 6, body, 0)
-
-    def theta_outer(step):
-        def body(k, carry):
-            sweep_theta(step, k + 4 * (k // 2))
-            return carry
-
-        lax.fori_loop(0, 4, body, 0)
-
     theta_inner(0)
     for tile in range(TILES + 1):
         for copy in tile_halos(tile, 0 if tile < middle else 1 if tile == middle else 2):
             copy.wait()
-    sweep_y_all(0, outer)
-    theta_outer(0)
-    for copy in second_halos():
-        copy.start()
-    sweep_y_all(1, inner)
+    for part in range(len(PARTS)):
+        sweep_y_of(0, ranges(*BEFORE[part]), outer)
+        theta_outer(0, *PARTS[part])
+        for copy in second_halos(part):
+            copy.start()
+    sweep_y_of(1, ranges(0, ND), inner)
     theta_inner(1)
-    for copy in second_halos():
-        copy.wait()
-    sweep_y_all(1, outer)
-    theta_outer(1)
 
     def collect(direction, tile, s):
-        taken = [lanes(y_buf[direction, v], take_at[v]) for v in range(ROWS)]
+        taken = [lanes(done[direction, v], take_at[v]) for v in range(ROWS)]
         for u in range(3):
             for h in range(2):
                 index = back_row[u, h]
@@ -594,10 +616,7 @@
                 for v in ROW_TILES[u]:
                     got = sublanes(taken[v], index)
                     value = got if value is None else jnp.where(which == v, got, value)
-                if s is None:
-                    p_buf[u, h, 120:128, :] = value
-                else:
-                    p_buf[tile, h, BUCKET * s + 8 * u : BUCKET * s + 8 * u + 8, :] = value
+                point_ref(tile, s, u, h)[...] = value
 
     def third_ends(tile, peer, early):
         source_ref = z_buf.at[tile, peer] if early else r_buf.at[tile, peer]
@@ -643,33 +662,45 @@
         source_ref, target_ref = back_ends(tile, me_c)
         return pltpu.make_async_copy(source_ref, target_ref, back_own.at[tile])
 
-    def collect_tile(early):
-        def body(tile, carry):
-            for s in range(FOLD):
-                collect(FOLD * tile + s, tile, s)
-            for h in range(2):
-                r_rows[tile, pl.ds(h, 128, stride=2), :] = p_buf[tile, h].T
-            if early:
-                for r in range(1, NC):
-                    back_copy(tile, r).start()
-                back_local(tile).start()
-            else:
-                third_send_all(tile, False)
-            return carry
-
-        return body
-
-    def back_tile_on(tile, carry):
+    def collect_tile(tile, early):
+        for s in range(FOLD):
+            collect(FOLD * tile + s, tile, s)
+        for h in range(2):
+            r_rows[tile, pl.ds(h, 128, stride=2), :] = p_buf[tile, h].T
+        if early:
+            for r in range(1, NC):
+                back_copy(tile, r).start()
+            back_local(tile).start()
+        else:
+            third_send_all(tile, False)
+
+    def back_tile_on(tile):
         cross_many(z_buf, tile, back_recv).wait()
         back_local(tile).wait()
         third_send_all(tile, True)
+
+    for part in range(len(PARTS)):
+        for copy in second_halos(part):
+            copy.wait()
+        sweep_y_of(1, SECOND_HALOS[part], outer)
+    theta_outer(1, 0, ND)
+
+    def collect_some(low, high, early):
+        def body(tile, carry):
+            collect_tile(tile, early)
+            return carry
+
+        lax.fori_loop(low, high, body, 0)
+
+    def back_on(tile, carry):
+        back_tile_on(tile)
         return carry
 
-    lax.fori_loop(EARLY, EARLY + 1, collect_tile(False), 0)
-    collect(LAST, None, None)
-    lax.fori_loop(0, EARLY, collect_tile(True), 0)
-    lax.fori_loop(EARLY + 1, TILES, collect_tile(False), 0)
-    lax.fori_loop(0, EARLY, back_tile_on, 0)
+    collect_some(EARLY, EARLY + 1, False)
+    collect(LAST, range(EARLY), None)
+    collect_some(0, EARLY, True)
+    collect_some(EARLY + 1, TILES, False)
+    lax.fori_loop(0, EARLY, back_on, 0)
 
     def put(direction, parts, early):
         for u in range(6):
@@ -787,6 +818,7 @@
             pltpu.VMEM((ND, NC, SLOTS), f32),
             pltpu.VMEM((2, ND, ROWS + 4) + vreg, f32),
             pltpu.VMEM((ND, ROWS) + vreg, f32),
+            pltpu.VMEM((ND, ROWS) + vreg, f32),
             pltpu.VMEM((64, 128), f32),
             pltpu.VMEM((64, 128), f32),
             pltpu.VMEM((64, 128), f32),
@@ -810,7 +842,7 @@
             dma((TILES,)), dma((TILES,)), dma((TILES,)),
             dma((EARLY,)), dma((EARLY,)), dma((EARLY,)),
             dma((EARLY,)), dma((EARLY,)), dma((EARLY,)),
-            dma((4,)), dma((4,)), dma((2, 2 * TILES + 2)), dma((2, 2 * TILES + 2)),
+            dma((4,)), dma((4,)), dma((2, HALOS)), dma((2, HALOS)),
             dma((TILES,)), dma((TILES,)), dma((TILES,)),
             dma((TILES,)), dma((TILES,)), dma((TILES,)),
         ],

time: 71.9 us -> 70.3 us (0.978)
  Pallas kernels: 70.7 us -> 69.1 us
    pallas_call x1, Pallas kernels: 70.7 us -> 69.1 us  [per_device(): pl.pallas_call(kernel, out_shape=pltpu.VMEM((ND, NC, SLOTS), f32), in_spe...]
where the time goes in v5:
time: 70.3 us; the launch traced here: 70.1 us
  Pallas kernels  69.1 us (98%)
  local copies, waits for them, and re-layouts  0.91 us (1%)
    pallas_call x1, Pallas kernels, per_device(): pl.pallas_call(kernel, out_shape=pltpu.VMEM((ND, NC, SLOTS), f32), in_spe...  69.1 us

profile of v5, /device:TPU:1, one launch (start us, length us, event | category | flops | bytes accessed | tf_op | source)
XLA Modules:
  0.0 70.1 jit_solution(17462816087663778001)
XLA Ops:
  0.0 69.1 %wave_step.1 = f32[36,8,768]{2,1,0:T(8,128)S(1)} custom-call(f32[36,8,768]{2,1,0:T(8,128)} %bitcast.4, f32[1,8,1024]{2,1,0:T(8,128)} %speed_in.1, f32[1,8,1024]{2,1,0:T(8,128)} %turn_in.1, s32[8,1024]{1,0:T(8,128)} %mask_in.1, s32[48,128]{1,0:T(8,128)} %bitcast.5, s32[32]{0:T(128)} %counts_in.1), custom_call_target="tpu_custom_call" | custom-call | tf_op jit(solution)/shard_map/wave_step/pallas_call | solution.py:797
  69.2 0.9 %copy.8 = f32[8,36,768]{2,0,1:T(8,128)} copy(f32[8,36,768]{2,0,1:T(8,128)S(1)} %bitcast.3) | data formatting | bytes 1769472

commit v6 on v5

--- a/solution.py
+++ b/solution.py
@@ -20,6 +20,7 @@
 LAST = ND - 1
 PARTS = ((0, 12), (12, 12), (24, 12))
 BEFORE = ((34, 16), (14, 12), (26, 8))
+ORDER = (4, 3, 2, 1, 8, 12, 5, 6, 7, 16, 20, 11, 10, 9, 24, 28, 13, 14, 15, 19, 18, 17, 21, 22, 23, 27, 26, 25, 29, 30, 31)
 SIN_POS = 19
 
 ANGLES = np.arange(ND, dtype=np.float32) * np.float32(2.0 * math.pi / ND)
@@ -367,7 +368,7 @@
                 first_wait(tile, first_recv).wait()
                 first_local(tile).wait()
                 pack(tile, False)
-            for r in range(1, NL):
+            for r in ORDER:
                 second_copy(tile, r, early).start()
             second_local(tile, early).start()
             return carry
@@ -564,11 +565,11 @@
 
     def theta_outer(step, first, number):
         def body(k, carry):
-            sweep_theta(step, first, number, k)
-            sweep_theta(step, first, number, k + 6)
+            for r in outer:
+                sweep_theta(step, first, number, r)
             return carry
 
-        lax.fori_loop(0, 2, body, 0)
+        lax.fori_loop(0, 1, body, 0)
 
     def receive_tile(kind):
         def body(tile, carry):
@@ -639,7 +640,7 @@
         return pltpu.make_async_copy(source_ref, target_ref, third_own.at[tile])
 
     def third_send_all(tile, early):
-        for r in range(1, NL):
+        for r in ORDER:
             third_copy(tile, r, early).start()
         third_local(tile, early).start()
 

time: 70.3 us -> 69.8 us (level)
  no operation moved by 1% of the time
where the time goes in v6:
time: 69.8 us; the launch traced here: 69.5 us
  Pallas kernels  68.6 us (98%)
  local copies, waits for them, and re-layouts  0.91 us (1%)
    pallas_call x1, Pallas kernels, per_device(): pl.pallas_call(kernel, out_shape=pltpu.VMEM((ND, NC, SLOTS), f32), in_spe...  68.6 us

profile of v6, /device:TPU:1, one launch (start us, length us, event | category | flops | bytes accessed | tf_op | source)
XLA Modules:
  0.0 69.5 jit_solution(18139312226781524860)
XLA Ops:
  0.0 68.6 %wave_step.1 = f32[36,8,768]{2,1,0:T(8,128)S(1)} custom-call(f32[36,8,768]{2,1,0:T(8,128)} %bitcast.4, f32[1,8,1024]{2,1,0:T(8,128)} %speed_in.1, f32[1,8,1024]{2,1,0:T(8,128)} %turn_in.1, s32[8,1024]{1,0:T(8,128)} %mask_in.1, s32[48,128]{1,0:T(8,128)} %bitcast.5, s32[32]{0:T(128)} %counts_in.1), custom_call_target="tpu_custom_call" | custom-call | tf_op jit(solution)/shard_map/wave_step/pallas_call | solution.py:798
  68.6 0.9 %copy.8 = f32[8,36,768]{2,0,1:T(8,128)} copy(f32[8,36,768]{2,0,1:T(8,128)S(1)} %bitcast.3) | data formatting | bytes 1769472
